TPU v7x, 128 devices: a whole 4x4x4 slice. The times are simulated.
128 devices in a mesh: grp: 8 (over x, core), dev: 16 (over z, y).
Axes of the slice: x: 4, y: 4, z: 4, core: 2. Of those that a mesh axis runs over, the one named last changes fastest.
Arguments:
- charges: bfloat16 [4096, 8, 256], P(('grp', 'dev')), may hold values from -6 to 6
- near_list: int32 [4096, 4], P(('grp', 'dev')), may hold values from 0 to 4095, as said below
- near_blocks: bfloat16 [4096, 4, 256, 256], P(('grp', 'dev')), may hold values from -0.1875 to 0.1875
- source_basis: bfloat16 [4096, 64, 256], P(('grp', 'dev')), may hold values from -0.375 to 0.375
- target_basis: bfloat16 [4096, 64, 256], P(('grp', 'dev')), may hold values from -0.75 to 0.75
- far_devices: int32 [4096, 8], P(('grp', 'dev')), may hold values from 0 to 127, all different within a row; in each aligned block of 32 rows (0 to 31, 32 to 63, ...) at most 4 rows name the same one
- far_slots: int32 [4096, 8], P(('grp', 'dev')), may hold values from 0 to 31
- far_couplings: bfloat16 [4096, 8, 64, 64], P(('grp', 'dev')), may hold values from -0.25 to 0.25
- up_transfer: bfloat16 [4096, 64, 64], P(('grp', 'dev')), may hold values from -0.125 to 0.125
- coarse_list: int32 [128, 6], P(('grp', 'dev')), may hold values from 0 to 127, as said below
- coarse_couplings: bfloat16 [128, 6, 64, 64], P(('grp', 'dev')), may hold values from -0.3125 to 0.3125
- down_transfer: bfloat16 [4096, 64, 64], P(('grp', 'dev')), may hold values from -0.75 to 0.75
Outputs:
- potentials: float32 [4096, 8, 256], P(('grp', 'dev'))
Inputs may be any that keep to these rules, and one draw needn't show every extreme that they name: `near_list`: entry 0 of leaf l is l itself, entry 1 is max(l - 32, 0), entry 2 is min(l + 32, 4095); every entry of leaf l lies within 32 leaves of l. `far_devices`: each row names 8 different devices; in the rows of one device (aligned blocks of 32 rows) no device is named more than 4 times. `coarse_list`: row n names 6 different nodes, none of them n, all of the same subtree as n: nodes m with m // 16 == n // 16.
All inputs are finite; a program needn't handle non-finite values.
Results may differ from a plain program's by a relative error of at most 0.0045.
Values may be sent and summed in bfloat16 or wider, within the bound.
No kernel may reach another device: no remote copies, remote signals or barrier semaphores. Data moves between devices by JAX's collectives and lax.ppermute only.
A program may use at most 128 MiB of HBM per device.

v0:
```python
import jax
import jax.numpy as jnp
from jax import lax
from jax.sharding import PartitionSpec as P


def with_halo(shard, sides, width):
    for axis, dim in sides:
        devices, length = (lax.axis_size(axis), shard.shape[dim])
        up = [(i, (i + 1) % devices) for i in range(devices - 1)]
        down = [(j, i) for i, j in up]
        last = lax.slice_in_dim(shard, length - width, length, axis=dim)
        leading = lax.slice_in_dim(shard, 0, width, axis=dim)
        before = lax.ppermute(last, axis, up)
        after = lax.ppermute(leading, axis, down)
        shard = jnp.concatenate([before, shard, after], axis=dim)
    return shard


def body(
    charges,
    near_list,
    near_blocks,
    source_basis,
    target_basis,
    far_devices,
    far_slots,
    far_couplings,
    up_transfer,
    coarse_list,
    coarse_couplings,
    down_transfer,
):
    leaves = charges.shape[0]
    right_sides = charges.shape[1]
    basis_rank = source_basis.shape[1]
    slot_width = right_sides * basis_rank
    far_count = far_devices.shape[1]
    per_group = lax.axis_size("dev")
    myself = lax.axis_index("grp") * per_group + lax.axis_index("dev")
    moments = jnp.einsum(
        "lkp,lrp->lrk", source_basis, charges, preferred_element_type=jnp.float32
    ).astype(jnp.bfloat16)
    extended = with_halo(charges, ((("grp", "dev"), 0),), leaves)
    offsets = near_list - (myself * leaves - leaves)
    sources = jnp.take(extended, offsets, axis=0)
    near_field = jnp.einsum(
        "ljpq,ljrq->lrp", near_blocks, sources, preferred_element_type=jnp.float32
    )
    products = jnp.einsum(
        "ljkq,lrq->ljrk", far_couplings, moments, preferred_element_type=jnp.float32
    )
    products = products.reshape(leaves * far_count, slot_width)
    target_device = far_devices.reshape(-1)
    target_slot = far_slots.reshape(-1)
    target_leaf = target_device * leaves + target_slot
    shifted = target_leaf
    inside = (shifted >= 0) & (shifted < leaves * lax.axis_size(("grp", "dev")))
    shifted = jnp.where(inside, shifted, leaves * lax.axis_size(("grp", "dev")))
    far_sum = lax.psum_scatter(
        jnp.zeros((leaves * lax.axis_size(("grp", "dev")), slot_width), jnp.float32)
        .at[shifted]
        .add(products, mode="drop"),
        ("grp", "dev"),
        scatter_dimension=0,
        tiled=True,
    )
    node_moment = jnp.einsum(
        "lkq,lrq->rk", up_transfer, moments, preferred_element_type=jnp.float32
    ).astype(jnp.bfloat16)
    subtree = lax.all_gather(node_moment[None], "dev", axis=0, tiled=True)
    picked = jnp.take(subtree, coarse_list[0] - lax.axis_index("grp") * per_group, axis=0)
    coarse_local = jnp.einsum(
        "jkq,jrq->rk", coarse_couplings[0], picked, preferred_element_type=jnp.float32
    ).astype(jnp.bfloat16)
    descended = jnp.einsum(
        "lkq,rq->lrk", down_transfer, coarse_local, preferred_element_type=jnp.float32
    )
    local_field = (far_sum.reshape(leaves, right_sides, basis_rank) + descended).astype(
        jnp.bfloat16
    )
    return near_field + jnp.einsum(
        "lkp,lrk->lrp", target_basis, local_field, preferred_element_type=jnp.float32
    )


def solution(mesh):
    return jax.shard_map(
        body,
        mesh=mesh,
        in_specs=(
            P(("grp", "dev"), None, None),
            P(("grp", "dev"), None),
            P(("grp", "dev"), None, None, None),
            P(("grp", "dev"), None, None),
            P(("grp", "dev"), None, None),
            P(("grp", "dev"), None),
            P(("grp", "dev"), None),
            P(("grp", "dev"), None, None, None),
            P(("grp", "dev"), None, None),
            P(("grp", "dev"), None),
            P(("grp", "dev"), None, None, None),
            P(("grp", "dev"), None, None),
        ),
        out_specs=P(("grp", "dev"), None, None),
        check_vma=False,
    )
```

profile of v0, /device:TPU:0, one launch (start us, length us, event | category | flops | bytes accessed | tf_op | source)
XLA Modules:
  0.0 684.0 jit_solution(4615899579989893898)
XLA Ops:
  6.5 0.0 copy-start
  6.5 0.8 multiply_add_fusion
  7.3 0.1 copy.17
  7.4 0.1 add.64
  7.5 1.7 convolution_convert_fusion
  9.2 5.5 convolution_bitcast_fusion
  14.7 0.3 reshape.108
  15.0 0.0 copy-start.3
  15.0 0.0 copy-start.4
  15.0 0.0 copy-start.6
  15.1 0.0 copy-start.2
  15.1 0.0 copy-start.5
  15.1 5.8 scatter_custom_fusion
  20.9 0.0 reduce-scatter.2.cloned.1.call-update
  20.9 1.3 collective-permute-start.1
  22.2 4.6 collective-permute-start
  26.8 0.1 copy.16
  26.9 0.1 reshape.90
  27.1 0.2 fusion.4
  27.3 0.1 copy.15
  27.4 27.3 %all-gather = bf16[128,64]{1,0:T(8,128)(2,1)S(1)} all-gather(bf16[8,64]{1,0:T(8,128)(2,1)S(1)} %fusion.4), channel_id=2, replica_groups=mesh['grp'=8,'dev'=16] {'dev'}, dimensions={0}, use_global_device_ids=true | all-gather | bytes 17408 | tf_op jit(solution)/shard_map/all_gather | solution.py:71
  54.7 0.6 gather_fusion.1
  55.3 0.2 fusion.6
  55.5 0.0 collective-permute-done.1
  55.5 0.0 collective-permute-done
  55.5 0.1 pad_maximum_fusion
  55.5 0.6 gather_fusion
  56.2 0.0 copy-start.1
  56.2 8.1 %convolution_bitcast_fusion.1 = f32[32,8,256]{2,1,0:T(8,128)S(1)} fusion(bf16[32,4,256,256]{3,2,1,0:T(8,128)(2,1)} %param.14, bf16[32,4,8,256]{3,2,1,0:T(8,128)(2,1)S(1)} %bitcast.53, pred[32,4]{1,0:T(8,128)(4,1)S(1)} %copy.15), kind=kOutput, calls=%fused_computation.7 | convolution fusion | flops 134479872 | bytes 17563776 | tf_op jit(solution)/shard_map/ljpq,ljrq->lrp/dot_general | solution.py:47
  64.3 610.5 %reduce-scatter.2.cloned.1.call-done = f32[32,512]{1,0:T(8,128)} async-done(((f32[4096,512]{1,0:T(8,128)}), f32[32,512]{1,0:T(8,128)}) %reduce-scatter.2.cloned.1.call-update) | async-done | bytes 65552 | tf_op jit(solution)/shard_map/reduce_scatter | solution.py:60
  674.8 0.9 reshape.87
  675.8 1.4 convolution_add_fusion
  (14 shorter events, 0.1 us)
Async XLA Ops:
  6.5 669.2 %copy-start = (bf16[32,64,256]{2,1,0:T(8,128)(2,1)S(1)}, bf16[32,64,256]{2,1,0:T(8,128)(2,1)}, u32[]{:S(2)}) copy-start(bf16[32,64,256]{2,1,0:T(8,128)(2,1)} %param.16) | copy-start | bytes 3145732
  6.5 668.3 %reduce-scatter.2.cloned.1.call-start = ((), (), s32[]{:S(2)}) async-start(), calls=%async_computation.1 | async-start | bytes 8454144 | tf_op jit(solution)/shard_map/reduce_scatter | solution.py:60
  15.0 5.9 copy-start.3
  15.0 11.8 %copy-start.4 = (s32[32,4]{0,1:T(4,128)S(1)}, s32[32,4]{0,1:T(4,128)}, u32[]{:S(2)}) copy-start(s32[32,4]{0,1:T(4,128)} %param.13) | copy-start | bytes 1540
  15.0 12.0 %copy-start.6 = (s32[1,6]{1,0:T(1,128)S(1)}, s32[1,6]{1,0:T(1,128)}, u32[]{:S(2)}) copy-start(s32[1,6]{1,0:T(1,128)} %param.21) | copy-start | bytes 76
  15.1 12.0 %copy-start.2 = (bf16[32,64,64]{2,1,0:T(8,128)(2,1)S(1)}, bf16[32,64,64]{2,1,0:T(8,128)(2,1)}, u32[]{:S(2)}) copy-start(bf16[32,64,64]{2,1,0:T(8,128)(2,1)} %param.20) | copy-start | bytes 786436
  15.1 40.2 %copy-start.5 = (bf16[1,6,64,64]{3,2,1,0:T(8,128)(2,1)S(1)}, bf16[1,6,64,64]{3,2,1,0:T(8,128)(2,1)}, u32[]{:S(2)}) copy-start(bf16[1,6,64,64]{3,2,1,0:T(8,128)(2,1)} %param.22) | copy-start | bytes 147460
  20.9 34.5 %collective-permute-start.1 = (bf16[32,8,256]{2,1,0:T(8,128)(2,1)S(1)}, bf16[32,8,256]{2,1,0:T(8,128)(2,1)S(1)}, u32[]{:S(2)}, u32[]{:S(2)}) collective-permute-start(bf16[32,8,256]{2,1,0:T(8,128)(2,1)S(1)} %copy-done.3), channel_id=1, source_target_pairs={{1,0},{2,1},{3,2},{4,3},{5,4},{6,5},{7,6},{8,7},{9,8},{10,9},{11,1... | collective-permute-start | bytes 393224 | tf_op jit(solution)/shard_map/ppermute | solution.py:15
  22.2 33.2 %collective-permute-start = (bf16[32,8,256]{2,1,0:T(8,128)(2,1)S(1)}, bf16[32,8,256]{2,1,0:T(8,128)(2,1)S(1)}, u32[]{:S(2)}, u32[]{:S(2)}) collective-permute-start(bf16[32,8,256]{2,1,0:T(8,128)(2,1)S(1)} %copy-done.3), channel_id=1, source_target_pairs={{0,1},{1,2},{2,3},{3,4},{4,5},{5,6},{6,7},{7,8},{8,9},{9,10},{10,1... | collective-permute-start | bytes 393224 | tf_op jit(solution)/shard_map/ppermute | solution.py:14
  56.2 619.5 %copy-start.1 = (bf16[32,64,64]{2,1,0:T(8,128)(2,1)S(1)}, bf16[32,64,64]{2,1,0:T(8,128)(2,1)}, u32[]{:S(2)}) copy-start(bf16[32,64,64]{2,1,0:T(8,128)(2,1)} %param.23) | copy-start | bytes 786436
Sparse Core Ops, SparseCore 0:
  21.0 653.7 reduce-scatter.1
where the time goes:
time: 684 us
  waiting for transfers between devices  610 us (89%)
  blocking collectives  27.3 us (4%)
  matrix products  17.1 us (3%)
  between operations  13.6 us (2%)
    reduce_scatter x1, waiting for transfers between devices, body(): lax.psum_scatter(jnp.zeros((leaves * lax.axis_size(('grp', 'dev')), slot_...  610 us
    all_gather x1, blocking collectives, body(): subtree = lax.all_gather(node_moment[None], 'dev', axis=0, tiled=True)  27.3 us
  transfers between devices with their start and end apart: 3, of which 1 were waited for; matrix products, arithmetic and copies ran while one was open for 1% of the time, Pallas kernels for 0%

commit v1 on v0

v1 whole, which is shorter than its diff:
```python
import jax
import jax.numpy as jnp
from jax import lax
from jax.experimental import pallas as pl
from jax.experimental.pallas import tpu as pltpu
from jax.sharding import PartitionSpec as P

AXES = ("grp", "dev")
LEAVES = 32
RHS = 8
RANK = 64
POINTS = 256
NFAR = 8
NNEAR = 4
NCOARSE = 6
DEVICES = 128
BF16 = jnp.bfloat16
F32 = jnp.float32
NT = (((1,), (1,)), ((), ()))
TN = (((0,), (0,)), ((), ()))
MIB = 1 << 20


def dot(a, b, dims=(((1,), (0,)), ((), ()))):
    return lax.dot_general(a, b, dims, preferred_element_type=F32)


def iota(shape, dim):
    return lax.broadcasted_iota(jnp.int32, shape, dim)


GROUP = 4


def in_hbm(*arrays):
    return tuple(pltpu.with_memory_space_constraint(array, pltpu.HBM) for array in arrays)


def outgoing_kernel(
    charges,
    devices,
    slots,
    basis,
    couplings,
    transfer,
    send,
    charges_v,
    devices_v,
    slots_v,
    basis_v,
    couplings_v,
    transfer_v,
    products,
    sems,
):
    steps = LEAVES // GROUP
    small = [
        pltpu.make_async_copy(src, dst, sems.at[3, i])
        for i, (src, dst) in enumerate(((charges, charges_v), (devices, devices_v), (slots, slots_v)))
    ]
    for copy in small:
        copy.start()
    copies = []
    for g in range(steps):
        part = pl.ds(g * GROUP, GROUP)
        copies.append(
            [
                pltpu.make_async_copy(src.at[part], dst.at[part], sems.at[i, g])
                for i, (src, dst) in enumerate(
                    ((basis, basis_v), (couplings, couplings_v), (transfer, transfer_v))
                )
            ]
        )
        for copy in copies[-1]:
            copy.start()
    for copy in small:
        copy.wait()

    entries = LEAVES * NFAR
    device = jnp.concatenate([devices_v[j : j + 1, :] for j in range(NFAR)], axis=1)
    slot = jnp.concatenate([slots_v[j : j + 1, :] for j in range(NFAR)], axis=1)
    named = iota((DEVICES, entries), 0) == device
    earlier = iota((entries, entries), 0) < iota((entries, entries), 1)
    counts = dot(named.astype(BF16), earlier.astype(BF16))
    order = jnp.sum(jnp.where(named, counts, 0.0), axis=0, keepdims=True).astype(jnp.int32)
    row_of = device * 8 + order
    slot_rows = jnp.broadcast_to((slot + 1).astype(F32), (128, entries)).astype(BF16)

    node = jnp.zeros((RHS, RANK), F32)
    for g in range(steps):
        for copy in copies[g]:
            copy.wait()
        at = g * GROUP
        rows = GROUP * RHS
        own = charges_v[at : at + GROUP].reshape(rows, POINTS)
        all_moments = dot(own, basis_v[at : at + GROUP].reshape(GROUP * RANK, POINTS), NT)
        moments = [
            all_moments[i * RHS : (i + 1) * RHS, i * RANK : (i + 1) * RANK].astype(BF16)
            for i in range(GROUP)
        ]
        raised = dot(
            jnp.concatenate(moments, axis=0), transfer_v[at : at + GROUP].reshape(GROUP * RANK, RANK), NT
        )
        for i in range(GROUP):
            node += raised[i * RHS : (i + 1) * RHS, i * RANK : (i + 1) * RANK]
            for h in range(2):
                half = couplings_v[at + i, h * 4 : h * 4 + 4].reshape(4 * RANK, RANK)
                product = dot(moments[i], half, NT)
                for t in range(2):
                    products[2 * h + t, (at + i) * RHS : (at + i + 1) * RHS, :] = product[
                        :, t * 128 : (t + 1) * 128
                    ]

    low = iota((LEAVES, 128), 1) < RANK
    pieces = []
    for c in range(4):
        piece = []
        for t in range(NFAR // 2):
            first = products[t, pl.ds(c, LEAVES, stride=RHS), :]
            second = products[t, pl.ds(c + 4, LEAVES, stride=RHS), :]
            piece.append(jnp.where(low, first, pltpu.roll(second, RANK, 1)))
            piece.append(jnp.where(low, pltpu.roll(first, RANK, 1), second))
        pieces.append(jnp.concatenate(piece, axis=0).astype(BF16))
    table = jnp.concatenate(
        [
            jnp.concatenate([pieces[0], pieces[2]], axis=1),
            jnp.concatenate([pieces[1], pieces[3]], axis=1),
        ],
        axis=0,
    )
    wide = jnp.concatenate([node, jnp.zeros((RHS, RANK), F32)], axis=1)
    turned = pltpu.roll(pltpu.roll(wide, RANK, 1), 4, 0)
    upper = iota((RHS, 128), 0) < 4
    node_rows = jnp.where(upper, jnp.where(iota((RHS, 128), 1) < RANK, wide, turned), 0.0)

    span = 256
    for at in range(0, DEVICES * 8, span):
        row = iota((span, entries), 0) + at
        chosen = (row == row_of).astype(BF16)
        second = (row == row_of + 4).astype(BF16)
        rows = dot(jnp.concatenate([chosen, second], axis=1), table)
        names = dot(second, slot_rows, NT).reshape(span // 8, 8, 128) + node_rows[None]
        part = pl.ds(at // 8, span // 8)
        send[part, 0] = rows[:, :128].reshape(span // 8, 8, 128).astype(BF16)
        send[part, 1] = rows[:, 128:].reshape(span // 8, 8, 128).astype(BF16)
        send[part, 2] = names.astype(BF16)


def outgoing(charges, far_devices, far_slots, source_basis, far_couplings, up_transfer):
    arrays = (charges, far_devices.T, far_slots.T, source_basis, far_couplings, up_transfer)
    return pl.pallas_call(
        outgoing_kernel,
        out_shape=jax.ShapeDtypeStruct((DEVICES, 3, 8, 128), BF16),
        in_specs=[pl.BlockSpec(memory_space=pltpu.HBM)] * 6,
        out_specs=pl.BlockSpec(memory_space=pltpu.VMEM),
        scratch_shapes=[pltpu.VMEM(array.shape, array.dtype) for array in arrays]
        + [
            pltpu.VMEM((NFAR // 2, LEAVES * RHS, 128), F32),
            pltpu.SemaphoreType.DMA((4, LEAVES // GROUP)),
        ],
        compiler_params=pltpu.CompilerParams(vmem_limit_bytes=24 * MIB),
        name="outgoing",
    )(*in_hbm(*arrays))


def near_kernel(near_list, base, charges, before, after, blocks, out, sources, blocks_v, sems):
    copies = []
    for g in range(LEAVES // GROUP):
        part = pl.ds(g * GROUP, GROUP)
        copies.append(pltpu.make_async_copy(blocks.at[part], blocks_v.at[part], sems.at[g]))
        copies[-1].start()
    sources[0:LEAVES] = before[...]
    sources[LEAVES : 2 * LEAVES] = charges[...]
    sources[2 * LEAVES : 3 * LEAVES] = after[...]
    half = POINTS // 2
    for g in range(LEAVES // GROUP):
        copies[g].wait()
        for l in range(g * GROUP, (g + 1) * GROUP):
            picked = [sources[near_list[j, l] - base[0]] for j in range(NNEAR)]
            for at in (0, half):
                terms = [dot(picked[j], blocks_v[l, j, at : at + half], NT) for j in range(NNEAR)]
                out[l, :, at : at + half] = sum(terms[1:], terms[0])


def near(near_list, base, charges, before, after, near_blocks):
    vmem = pl.BlockSpec(memory_space=pltpu.VMEM)
    smem = pl.BlockSpec(memory_space=pltpu.SMEM)
    hbm = pl.BlockSpec(memory_space=pltpu.HBM)
    return pl.pallas_call(
        near_kernel,
        out_shape=jax.ShapeDtypeStruct((LEAVES, RHS, POINTS), F32),
        in_specs=[smem, smem, vmem, vmem, vmem, hbm],
        out_specs=vmem,
        scratch_shapes=[
            pltpu.VMEM((3 * LEAVES, RHS, POINTS), BF16),
            pltpu.VMEM(near_blocks.shape, BF16),
            pltpu.SemaphoreType.DMA((LEAVES // GROUP,)),
        ],
        compiler_params=pltpu.CompilerParams(vmem_limit_bytes=32 * MIB),
        cost_estimate=pl.CostEstimate(flops=268435456, bytes_accessed=17000000, transcendentals=0),
        name="near",
    )(near_list.T, base, charges, before, after, *in_hbm(near_blocks))


def unfold(rows):
    return jnp.concatenate([rows[:, :RANK], rows[:, RANK:]], axis=0)


def final_kernel(coarse_list, recv, near_field, target_basis, couplings, transfer, out):
    coarse = jnp.zeros((RHS, RANK), F32)
    for j in range(NCOARSE):
        picked = unfold(recv[coarse_list[0, j], 2].astype(F32)[:4]).astype(BF16)
        coarse += dot(picked, couplings[0, j], NT)
    lowered = dot(coarse.astype(BF16), transfer[...].reshape(LEAVES * RANK, RANK), NT)

    far = jnp.zeros((128, 128), F32)
    span = 32
    lane = iota((span, 8, 128), 2)
    place = iota((span, 8, 128), 1)
    for at in range(0, DEVICES, span):
        part = pl.ds(at, span)
        names = recv[part, 2].astype(F32)
        names = jnp.where(place >= 4, names, pltpu.roll(names, 4, 1)).astype(jnp.int32) - 1
        same = names == lane // 4
        for g in range(2):
            chosen = (same & (lane % 4 == 2 * g + place // 4)).astype(F32)
            far += dot(
                chosen.reshape(span * 8, 128).astype(BF16), recv[part, g].reshape(span * 8, 128), TN
            )
    for l in range(LEAVES):
        rows = unfold(far[l * 4 : (l + 1) * 4, :])
        local = (rows + lowered[:, l * RANK : (l + 1) * RANK]).astype(BF16)
        out[l] = near_field[l] + dot(local, target_basis[l])


def final(coarse_list, recv, near_field, target_basis, coarse_couplings, down_transfer):
    vmem = pl.BlockSpec(memory_space=pltpu.VMEM)
    smem = pl.BlockSpec(memory_space=pltpu.SMEM)
    return pl.pallas_call(
        final_kernel,
        out_shape=jax.ShapeDtypeStruct((LEAVES, RHS, POINTS), F32),
        in_specs=[smem, vmem, vmem, vmem, vmem, vmem],
        out_specs=vmem,
        compiler_params=pltpu.CompilerParams(vmem_limit_bytes=24 * MIB),
        name="final",
    )(coarse_list, recv, near_field, target_basis, coarse_couplings, down_transfer)


def body(
    charges,
    near_list,
    near_blocks,
    source_basis,
    target_basis,
    far_devices,
    far_slots,
    far_couplings,
    up_transfer,
    coarse_list,
    coarse_couplings,
    down_transfer,
):
    count = lax.axis_size(AXES)
    myself = lax.axis_index(AXES)
    up = [(i, i + 1) for i in range(count - 1)]
    down = [(j, i) for i, j in up]
    send = outgoing(charges, far_devices, far_slots, source_basis, far_couplings, up_transfer)
    before = lax.ppermute(charges, AXES, up)
    after = lax.ppermute(charges, AXES, down)
    send, before, after = lax.optimization_barrier((send, before, after))
    recv = lax.all_to_all(send, AXES, 0, 0, tiled=True)
    base = jnp.full((1,), myself * LEAVES - LEAVES, jnp.int32)
    near_field = near(near_list, base, charges, before, after, near_blocks)
    return final(coarse_list, recv, near_field, target_basis, coarse_couplings, down_transfer)


def solution(mesh):
    return jax.shard_map(
        body,
        mesh=mesh,
        in_specs=(P(AXES),) * 12,
        out_specs=P(AXES),
        check_vma=False,
    )
```

time: 684 us -> 43.9 us (0.06)
  the two profiles are of different devices: /device:TPU:0 before, /device:TPU:1 now
where the time goes in v1:
time: 43.9 us; the launch traced here: 43.6 us
  starting transfers between devices  17.5 us (40%)
  Pallas kernels  16.9 us (38%)
  waiting for transfers between devices  7.55 us (17%)
  local copies, waits for them, and re-layouts  1.6 us (4%)
    all_to_all x1, waiting for transfers between devices, body(): recv = lax.all_to_all(send, AXES, 0, 0, tiled=True)  7.54 us
    pallas_call x1, Pallas kernels, near(): pl.pallas_call(near_kernel, out_shape=jax.ShapeDtypeStruct((LEAVES, RHS,...  7.51 us
    ppermute x1, starting transfers between devices, body(): after = lax.ppermute(charges, AXES, down)  7.39 us
    pallas_call x1, Pallas kernels, outgoing(): pl.pallas_call(outgoing_kernel, out_shape=jax.ShapeDtypeStruct((DEVICES,...  7.12 us
    all_to_all x1, starting transfers between devices, body(): recv = lax.all_to_all(send, AXES, 0, 0, tiled=True)  5.92 us
    ppermute x1, starting transfers between devices, body(): before = lax.ppermute(charges, AXES, up)  4.17 us
    pallas_call x1, Pallas kernels, final(): pl.pallas_call(final_kernel, out_shape=jax.ShapeDtypeStruct((LEAVES, RHS,...  2.27 us
    unnamed x12, local copies, waits for them, and re-layouts  1.6 us
  transfers between devices with their start and end apart: 3, of which 1 were waited for; matrix products, arithmetic and copies ran while one was open for 0% of the time, Pallas kernels for 34%

profile of v1, /device:TPU:1, one launch (start us, length us, event | category | flops | bytes accessed | tf_op | source)
XLA Modules:
  0.0 43.6 jit_solution(8718476859823425697)
XLA Ops:
  0.0 0.0 copy-start
  0.0 0.0 copy-start.5
  0.0 0.0 copy-start.3
  0.0 0.0 copy-start.2
  0.0 4.2 %collective-permute-start = (bf16[32,8,256]{2,1,0:T(8,128)(2,1)}, bf16[32,8,256]{2,1,0:T(8,128)(2,1)S(1)}, u32[]{:S(2)}, u32[]{:S(2)}) collective-permute-start(bf16[32,8,256]{2,1,0:T(8,128)(2,1)} %charges.3), channel_id=1, source_target_pairs={{0,1},{1,2},{2,3},{3,4},{4,5},{5,6},{6,7},{7,8},{8,9},{9,10},{10,1... | collective-permute-start | bytes 393224 | tf_op jit(solution)/shard_map/ppermute | solution.py:268
  4.2 7.4 %collective-permute-start.1 = (bf16[32,8,256]{2,1,0:T(8,128)(2,1)}, bf16[32,8,256]{2,1,0:T(8,128)(2,1)S(1)}, u32[]{:S(2)}, u32[]{:S(2)}) collective-permute-start(bf16[32,8,256]{2,1,0:T(8,128)(2,1)} %charges.3), channel_id=1, source_target_pairs={{1,0},{2,1},{3,2},{4,3},{5,4},{6,5},{7,6},{8,7},{9,8},{10,9},{11,1... | collective-permute-start | bytes 393224 | tf_op jit(solution)/shard_map/ppermute | solution.py:269
  11.6 7.1 %outgoing.1 = bf16[128,3,8,128]{3,2,1,0:T(8,128)(2,1)} custom-call(bf16[32,8,256]{2,1,0:T(8,128)(2,1)} %charges.3, s32[8,32]{1,0:T(8,128)} %bitcast.5, s32[8,32]{1,0:T(8,128)} %bitcast.6, bf16[32,64,256]{2,1,0:T(8,128)(2,1)} %basis.1, bf16[32,8,64,64]{3,2,1,0:T(8,128)(2,1)} %couplings.2, bf16[32,64,64]{2,1,0:T(8,128)(2,1)} %transfer.2), custom_call_target="tpu_custom_call" | custom-call | tf_op jit(solution)/shard_map/outgoing/pallas_call | solution.py:151
  18.7 0.0 collective-permute-done.before
  18.7 0.0 collective-permute-done.1.after
  18.7 5.9 %all-to-all-start = ((bf16[128,3,8,128]{3,2,1,0:T(8,128)(2,1)}), bf16[128,3,8,128]{3,2,1,0:T(8,128)(2,1)S(1)}, u32[]{:S(2)}, u32[]{:S(2)}) async-start(bf16[128,3,8,128]{3,2,1,0:T(8,128)(2,1)} %outgoing.1), calls=%async_computation | async-start | bytes 1572864 | tf_op jit(solution)/shard_map/all_to_all | solution.py:271
  24.7 0.0 copy-start.1
  24.7 0.9 %copy-done.1 = bf16[32,8,256]{2,1,0:T(8,128)(2,1)S(1)} copy-done((bf16[32,8,256]{2,1,0:T(8,128)(2,1)S(1)}, bf16[32,8,256]{2,1,0:T(8,128)(2,1)}, u32[]{:S(2)}) %copy-start.1) | copy-done | bytes 131096
  25.6 0.0 copy-start.4
  25.6 0.7 %copy-done.4 = s32[32,4]{0,1:T(4,128)S(1)} copy-done((s32[32,4]{0,1:T(4,128)S(1)}, s32[32,4]{0,1:T(4,128)}, u32[]{:S(2)}) %copy-start.4) | copy-done | bytes 536
  26.3 7.5 %near.1.near_field = f32[32,8,256]{2,1,0:T(8,128)S(1)} custom-call(s32[4,32]{1,0:T(4,128)S(1)} %bitcast.4, s32[1]{0:T(128)} %bitcast.3.base, bf16[32,8,256]{2,1,0:T(8,128)(2,1)S(1)} %copy-done.1, bf16[32,8,256]{2,1,0:T(8,128)(2,1)S(1)} %collective-permute-done.before, bf16[32,8,256]{2,1,0:T(8,128)(2,1)S(1)} %collective-permute-done.1.after, ...), custom_call_target="tpu_custom_call" | custom-call | flops 268435456 | bytes 17000000 | tf_op jit(solution)/shard_map/near/pallas_call | solution.py:189
  33.8 7.5 %all-to-all-done.recv = bf16[128,3,8,128]{3,2,1,0:T(8,128)(2,1)S(1)} async-done(((bf16[128,3,8,128]{3,2,1,0:T(8,128)(2,1)}), bf16[128,3,8,128]{3,2,1,0:T(8,128)(2,1)S(1)}, u32[]{:S(2)}, u32[]{:S(2)}) %all-to-all-start) | async-done | bytes 786464 | tf_op jit(solution)/shard_map/all_to_all | solution.py:271
  41.3 0.0 copy-done
  41.3 0.0 copy-done.5
  41.3 0.0 copy-done.3
  41.3 0.0 copy-done.2
  41.4 2.3 %final.1 = f32[32,8,256]{2,1,0:T(8,128)} custom-call(s32[1,6]{1,0:T(1,128)S(1)} %copy-done.5, bf16[128,3,8,128]{3,2,1,0:T(8,128)(2,1)S(1)} %all-to-all-done.recv, f32[32,8,256]{2,1,0:T(8,128)S(1)} %near.1.near_field, bf16[32,64,256]{2,1,0:T(8,128)(2,1)S(1)} %copy-done, bf16[1,6,64,64]{3,2,1,0:T(8,128)(2,1)S(1)} %copy-done.3, bf16[32,64,64]{2,1,0:T(8,128)(2,1)S(1)} %copy-done.2), custom_call_target="tpu_custom_call" | custom-call | tf_op jit(solution)/shard_map/final/pallas_call | solution.py:239
Async XLA Ops:
  0.0 41.3 %copy-start = (bf16[32,64,256]{2,1,0:T(8,128)(2,1)S(1)}, bf16[32,64,256]{2,1,0:T(8,128)(2,1)}, u32[]{:S(2)}) copy-start(bf16[32,64,256]{2,1,0:T(8,128)(2,1)} %target_basis.1) | copy-start | bytes 3145732
  0.0 41.3 %copy-start.5 = (s32[1,6]{1,0:T(1,128)S(1)}, s32[1,6]{1,0:T(1,128)}, u32[]{:S(2)}) copy-start(s32[1,6]{1,0:T(1,128)} %coarse_list.1) | copy-start | bytes 76
  0.0 41.3 %copy-start.3 = (bf16[1,6,64,64]{3,2,1,0:T(8,128)(2,1)S(1)}, bf16[1,6,64,64]{3,2,1,0:T(8,128)(2,1)}, u32[]{:S(2)}) copy-start(bf16[1,6,64,64]{3,2,1,0:T(8,128)(2,1)} %couplings.3) | copy-start | bytes 147460
  0.0 41.3 %copy-start.2 = (bf16[32,64,64]{2,1,0:T(8,128)(2,1)S(1)}, bf16[32,64,64]{2,1,0:T(8,128)(2,1)}, u32[]{:S(2)}) copy-start(bf16[32,64,64]{2,1,0:T(8,128)(2,1)} %transfer.3) | copy-start | bytes 786436
  0.0 18.7 %collective-permute-start = (bf16[32,8,256]{2,1,0:T(8,128)(2,1)}, bf16[32,8,256]{2,1,0:T(8,128)(2,1)S(1)}, u32[]{:S(2)}, u32[]{:S(2)}) collective-permute-start(bf16[32,8,256]{2,1,0:T(8,128)(2,1)} %charges.3), channel_id=1, source_target_pairs={{0,1},{1,2},{2,3},{3,4},{4,5},{5,6},{6,7},{7,8},{8,9},{9,10},{10,1... | collective-permute-start | bytes 393224 | tf_op jit(solution)/shard_map/ppermute | solution.py:268
  4.2 14.5 %collective-permute-start.1 = (bf16[32,8,256]{2,1,0:T(8,128)(2,1)}, bf16[32,8,256]{2,1,0:T(8,128)(2,1)S(1)}, u32[]{:S(2)}, u32[]{:S(2)}) collective-permute-start(bf16[32,8,256]{2,1,0:T(8,128)(2,1)} %charges.3), channel_id=1, source_target_pairs={{1,0},{2,1},{3,2},{4,3},{5,4},{6,5},{7,6},{8,7},{9,8},{10,9},{11,1... | collective-permute-start | bytes 393224 | tf_op jit(solution)/shard_map/ppermute | solution.py:269
  18.7 22.6 %all-to-all-start = ((bf16[128,3,8,128]{3,2,1,0:T(8,128)(2,1)}), bf16[128,3,8,128]{3,2,1,0:T(8,128)(2,1)S(1)}, u32[]{:S(2)}, u32[]{:S(2)}) async-start(bf16[128,3,8,128]{3,2,1,0:T(8,128)(2,1)} %outgoing.1), calls=%async_computation | async-start | bytes 1572864 | tf_op jit(solution)/shard_map/all_to_all | solution.py:271
  24.7 0.9 %copy-start.1 = (bf16[32,8,256]{2,1,0:T(8,128)(2,1)S(1)}, bf16[32,8,256]{2,1,0:T(8,128)(2,1)}, u32[]{:S(2)}) copy-start(bf16[32,8,256]{2,1,0:T(8,128)(2,1)} %charges.3) | copy-start | bytes 393220
  25.6 0.7 %copy-start.4 = (s32[32,4]{0,1:T(4,128)S(1)}, s32[32,4]{0,1:T(4,128)}, u32[]{:S(2)}) copy-start(s32[32,4]{0,1:T(4,128)} %param.13) | copy-start | bytes 1540

commit v2 on v1

--- a/solution.py
+++ b/solution.py
@@ -19,6 +19,8 @@
 NT = (((1,), (1,)), ((), ()))
 TN = (((0,), (0,)), ((), ()))
 MIB = 1 << 20
+NEAR_FLOPS = 26843545600
+NEAR_BYTES = 170000000
 
 
 def dot(a, b, dims=(((1,), (0,)), ((), ()))):
@@ -30,6 +32,7 @@
 
 
 GROUP = 4
+CHUNKS = ((0, 16), (16, 32))
 
 
 def in_hbm(*arrays):
@@ -51,30 +54,31 @@
     couplings_v,
     transfer_v,
     products,
+    chosen,
     sems,
 ):
-    steps = LEAVES // GROUP
     small = [
-        pltpu.make_async_copy(src, dst, sems.at[3, i])
-        for i, (src, dst) in enumerate(((charges, charges_v), (devices, devices_v), (slots, slots_v)))
+        pltpu.make_async_copy(src, dst, sems.at[i])
+        for i, (src, dst) in enumerate(
+            (
+                (charges, charges_v),
+                (basis, basis_v),
+                (devices, devices_v),
+                (slots, slots_v),
+                (transfer, transfer_v),
+            )
+        )
     ]
     for copy in small:
         copy.start()
-    copies = []
-    for g in range(steps):
-        part = pl.ds(g * GROUP, GROUP)
-        copies.append(
-            [
-                pltpu.make_async_copy(src.at[part], dst.at[part], sems.at[i, g])
-                for i, (src, dst) in enumerate(
-                    ((basis, basis_v), (couplings, couplings_v), (transfer, transfer_v))
-                )
-            ]
-        )
-        for copy in copies[-1]:
-            copy.start()
-    for copy in small:
-        copy.wait()
+    copies = [
+        pltpu.make_async_copy(couplings.at[low:high], couplings_v.at[low:high], sems.at[len(small) + g])
+        for g, (low, high) in enumerate(CHUNKS)
+    ]
+    for copy in copies:
+        copy.start()
+    small[2].wait()
+    small[3].wait()
 
     entries = LEAVES * NFAR
     device = jnp.concatenate([devices_v[j : j + 1, :] for j in range(NFAR)], axis=1)
@@ -85,31 +89,48 @@
     order = jnp.sum(jnp.where(named, counts, 0.0), axis=0, keepdims=True).astype(jnp.int32)
     row_of = device * 8 + order
     slot_rows = jnp.broadcast_to((slot + 1).astype(F32), (128, entries)).astype(BF16)
-
-    node = jnp.zeros((RHS, RANK), F32)
-    for g in range(steps):
-        for copy in copies[g]:
-            copy.wait()
-        at = g * GROUP
-        rows = GROUP * RHS
-        own = charges_v[at : at + GROUP].reshape(rows, POINTS)
-        all_moments = dot(own, basis_v[at : at + GROUP].reshape(GROUP * RANK, POINTS), NT)
-        moments = [
-            all_moments[i * RHS : (i + 1) * RHS, i * RANK : (i + 1) * RANK].astype(BF16)
-            for i in range(GROUP)
-        ]
-        raised = dot(
-            jnp.concatenate(moments, axis=0), transfer_v[at : at + GROUP].reshape(GROUP * RANK, RANK), NT
+    span = 256
+    for at in range(0, DEVICES * 8, span):
+        row = iota((span, entries), 0) + at
+        chosen[at : at + span, :entries] = (row == row_of).astype(BF16)
+        chosen[at : at + span, entries:] = (row == row_of + 4).astype(BF16)
+
+    small[0].wait()
+    small[1].wait()
+    moments = []
+    for at in range(0, LEAVES, 4):
+        own = charges_v[at : at + 4].reshape(4 * RHS, POINTS)
+        product = dot(own, basis_v[at : at + 4].reshape(4 * RANK, POINTS), NT)
+        for i in range(4):
+            moments.append(product[i * RHS : (i + 1) * RHS, i * RANK : (i + 1) * RANK].astype(BF16))
+    small[4].wait()
+    raised = []
+    for at in range(0, LEAVES, 4):
+        product = dot(
+            jnp.concatenate(moments[at : at + 4], axis=0),
+            transfer_v[at : at + 4].reshape(4 * RANK, RANK),
+            NT,
         )
-        for i in range(GROUP):
-            node += raised[i * RHS : (i + 1) * RHS, i * RANK : (i + 1) * RANK]
+        raised += [product[i * RHS : (i + 1) * RHS, i * RANK : (i + 1) * RANK] for i in range(4)]
+    while len(raised) > 1:
+        raised = [a + b for a, b in zip(raised[::2], raised[1::2])]
+    node = raised[0]
+    wide = jnp.concatenate([node, jnp.zeros((RHS, RANK), F32)], axis=1)
+    turned = pltpu.roll(pltpu.roll(wide, RANK, 1), 4, 0)
+    upper = iota((RHS, 128), 0) < 4
+    node_rows = jnp.where(upper, jnp.where(iota((RHS, 128), 1) < RANK, wide, turned), 0.0)
+    for at in range(0, DEVICES * 8, span):
+        names = dot(chosen[at : at + span, entries:], slot_rows, NT).reshape(span // 8, 8, 128)
+        send[at // 8 : (at + span) // 8, 2] = (names + node_rows[None]).astype(BF16)
+
+    for copy, (low, high) in zip(copies, CHUNKS):
+        copy.wait()
+        for l in range(low, high):
             for h in range(2):
-                half = couplings_v[at + i, h * 4 : h * 4 + 4].reshape(4 * RANK, RANK)
-                product = dot(moments[i], half, NT)
+                half = couplings_v[l, h * 4 : h * 4 + 4].reshape(4 * RANK, RANK)
+                product = dot(moments[l], half, NT)
                 for t in range(2):
-                    products[2 * h + t, (at + i) * RHS : (at + i + 1) * RHS, :] = product[
-                        :, t * 128 : (t + 1) * 128
-                    ]
+                    products[2 * h + t, l * RHS : (l + 1) * RHS, :] = product[:, t * 128 : (t + 1) * 128]
 
     low = iota((LEAVES, 128), 1) < RANK
     pieces = []
@@ -128,22 +149,11 @@
         ],
         axis=0,
     )
-    wide = jnp.concatenate([node, jnp.zeros((RHS, RANK), F32)], axis=1)
-    turned = pltpu.roll(pltpu.roll(wide, RANK, 1), 4, 0)
-    upper = iota((RHS, 128), 0) < 4
-    node_rows = jnp.where(upper, jnp.where(iota((RHS, 128), 1) < RANK, wide, turned), 0.0)
-
-    span = 256
     for at in range(0, DEVICES * 8, span):
-        row = iota((span, entries), 0) + at
-        chosen = (row == row_of).astype(BF16)
-        second = (row == row_of + 4).astype(BF16)
-        rows = dot(jnp.concatenate([chosen, second], axis=1), table)
-        names = dot(second, slot_rows, NT).reshape(span // 8, 8, 128) + node_rows[None]
+        rows = dot(chosen[at : at + span, :], table)
         part = pl.ds(at // 8, span // 8)
         send[part, 0] = rows[:, :128].reshape(span // 8, 8, 128).astype(BF16)
         send[part, 1] = rows[:, 128:].reshape(span // 8, 8, 128).astype(BF16)
-        send[part, 2] = names.astype(BF16)
 
 
 def outgoing(charges, far_devices, far_slots, source_basis, far_couplings, up_transfer):
@@ -156,50 +166,56 @@
         scratch_shapes=[pltpu.VMEM(array.shape, array.dtype) for array in arrays]
         + [
             pltpu.VMEM((NFAR // 2, LEAVES * RHS, 128), F32),
-            pltpu.SemaphoreType.DMA((4, LEAVES // GROUP)),
+            pltpu.VMEM((DEVICES * 8, 2 * LEAVES * NFAR), BF16),
+            pltpu.SemaphoreType.DMA((5 + len(CHUNKS),)),
         ],
         compiler_params=pltpu.CompilerParams(vmem_limit_bytes=24 * MIB),
+        cost_estimate=pl.CostEstimate(flops=2684354560, bytes_accessed=60000000, transcendentals=0),
         name="outgoing",
     )(*in_hbm(*arrays))
 
 
-def near_kernel(near_list, base, charges, before, after, blocks, out, sources, blocks_v, sems):
+def near_kernel(near_list, place, charges, first, second, blocks, out, sources, blocks_v, sems):
+    own = pltpu.make_async_copy(charges, sources.at[pl.ds(LEAVES, LEAVES)], sems.at[LEAVES // GROUP])
+    own.start()
     copies = []
     for g in range(LEAVES // GROUP):
         part = pl.ds(g * GROUP, GROUP)
         copies.append(pltpu.make_async_copy(blocks.at[part], blocks_v.at[part], sems.at[g]))
         copies[-1].start()
-    sources[0:LEAVES] = before[...]
-    sources[LEAVES : 2 * LEAVES] = charges[...]
-    sources[2 * LEAVES : 3 * LEAVES] = after[...]
+    base, parity = place[0], place[1]
+    sources[pl.ds((1 - parity) * 2 * LEAVES, LEAVES)] = first[...]
+    sources[pl.ds(parity * 2 * LEAVES, LEAVES)] = second[...]
+    own.wait()
     half = POINTS // 2
     for g in range(LEAVES // GROUP):
         copies[g].wait()
         for l in range(g * GROUP, (g + 1) * GROUP):
-            picked = [sources[near_list[j, l] - base[0]] for j in range(NNEAR)]
+            picked = [sources[near_list[j, l] - base] for j in range(NNEAR)]
             for at in (0, half):
                 terms = [dot(picked[j], blocks_v[l, j, at : at + half], NT) for j in range(NNEAR)]
                 out[l, :, at : at + half] = sum(terms[1:], terms[0])
 
 
-def near(near_list, base, charges, before, after, near_blocks):
+def near(near_list, place, charges, first, second, near_blocks):
     vmem = pl.BlockSpec(memory_space=pltpu.VMEM)
     smem = pl.BlockSpec(memory_space=pltpu.SMEM)
     hbm = pl.BlockSpec(memory_space=pltpu.HBM)
+    near_list, charges, near_blocks = in_hbm(near_list.T, charges, near_blocks)
     return pl.pallas_call(
         near_kernel,
         out_shape=jax.ShapeDtypeStruct((LEAVES, RHS, POINTS), F32),
-        in_specs=[smem, smem, vmem, vmem, vmem, hbm],
+        in_specs=[smem, smem, hbm, vmem, vmem, hbm],
         out_specs=vmem,
         scratch_shapes=[
             pltpu.VMEM((3 * LEAVES, RHS, POINTS), BF16),
             pltpu.VMEM(near_blocks.shape, BF16),
-            pltpu.SemaphoreType.DMA((LEAVES // GROUP,)),
+            pltpu.SemaphoreType.DMA((LEAVES // GROUP + 1,)),
         ],
         compiler_params=pltpu.CompilerParams(vmem_limit_bytes=32 * MIB),
-        cost_estimate=pl.CostEstimate(flops=268435456, bytes_accessed=17000000, transcendentals=0),
+        cost_estimate=pl.CostEstimate(flops=NEAR_FLOPS, bytes_accessed=NEAR_BYTES, transcendentals=0),
         name="near",
-    )(near_list.T, base, charges, before, after, *in_hbm(near_blocks))
+    )(near_list, place, charges, first, second, near_blocks)
 
 
 def unfold(rows):
@@ -262,15 +278,14 @@
 ):
     count = lax.axis_size(AXES)
     myself = lax.axis_index(AXES)
-    up = [(i, i + 1) for i in range(count - 1)]
-    down = [(j, i) for i, j in up]
+    pairs = [[(i, i + 1) for i in range(start, count - 1, 2)] for start in (0, 1)]
+    first, second = [
+        lax.ppermute(charges, AXES, some + [(j, i) for i, j in some]) for some in pairs
+    ]
     send = outgoing(charges, far_devices, far_slots, source_basis, far_couplings, up_transfer)
-    before = lax.ppermute(charges, AXES, up)
-    after = lax.ppermute(charges, AXES, down)
-    send, before, after = lax.optimization_barrier((send, before, after))
     recv = lax.all_to_all(send, AXES, 0, 0, tiled=True)
-    base = jnp.full((1,), myself * LEAVES - LEAVES, jnp.int32)
-    near_field = near(near_list, base, charges, before, after, near_blocks)
+    place = jnp.stack([myself * LEAVES - LEAVES, myself % 2])
+    near_field = near(near_list, place, charges, first, second, near_blocks)
     return final(coarse_list, recv, near_field, target_basis, coarse_couplings, down_transfer)
 
 

time: 43.9 us -> 40.3 us (0.918)
  starting transfers between devices: 17.5 us -> 15.9 us
  Pallas kernels: 16.9 us -> 15.3 us
  local copies, waits for them, and re-layouts: 1.6 us -> 0.02 us
  waiting for transfers between devices: 7.55 us -> 8.66 us
    pallas_call x1, Pallas kernels: 7.12 us -> 5.2 us  [outgoing(): pl.pallas_call(outgoing_kernel, out_shape=jax.ShapeDtypeStruct((DEVICES,...]
    unnamed x12 -> x8, local copies, waits for them, and re-layouts: 1.6 us -> 0.02 us
    ppermute x2, starting transfers between devices: 11.6 us -> 10.2 us  [body(): lax.ppermute(charges, AXES, some + [(j, i) for i, j in some])]
    all_to_all x1, waiting for transfers between devices: 7.54 us -> 8.66 us  [body(): recv = lax.all_to_all(send, AXES, 0, 0, tiled=True)]
  transfers between devices with their start and end apart: 3 -> 3, of which waited for: 1 -> 1; matrix products, arithmetic and copies ran while one was open for 0% -> 0% of each run, Pallas kernels for 34% -> 33%
where the time goes in v2:
time: 40.3 us; the launch traced here: 40.1 us
  starting transfers between devices  15.9 us (39%)
  Pallas kernels  15.3 us (38%)
  waiting for transfers between devices  8.66 us (21%)
    ppermute x2, starting transfers between devices, body(): lax.ppermute(charges, AXES, some + [(j, i) for i, j in some])  10.2 us
    all_to_all x1, waiting for transfers between devices, body(): recv = lax.all_to_all(send, AXES, 0, 0, tiled=True)  8.66 us
    pallas_call x1, Pallas kernels, near(): pl.pallas_call(near_kernel, out_shape=jax.ShapeDtypeStruct((LEAVES, RHS,...  7.86 us
    all_to_all x1, starting transfers between devices, body(): recv = lax.all_to_all(send, AXES, 0, 0, tiled=True)  5.66 us
    pallas_call x1, Pallas kernels, outgoing(): pl.pallas_call(outgoing_kernel, out_shape=jax.ShapeDtypeStruct((DEVICES,...  5.2 us
    pallas_call x1, Pallas kernels, final(): pl.pallas_call(final_kernel, out_shape=jax.ShapeDtypeStruct((LEAVES, RHS,...  2.27 us
  transfers between devices with their start and end apart: 3, of which 1 were waited for; matrix products, arithmetic and copies ran while one was open for 0% of the time, Pallas kernels for 33%

profile of v2, /device:TPU:1, one launch (start us, length us, event | category | flops | bytes accessed | tf_op | source)
XLA Modules:
  0.0 40.1 jit_solution(13322876736571033891)
XLA Ops:
  0.0 2.1 %collective-permute-start = (bf16[32,8,256]{2,1,0:T(8,128)(2,1)}, bf16[32,8,256]{2,1,0:T(8,128)(2,1)S(1)}, u32[]{:S(2)}, u32[]{:S(2)}) collective-permute-start(bf16[32,8,256]{2,1,0:T(8,128)(2,1)} %charges.3), channel_id=1, source_target_pairs={{0,1},{2,3},{4,5},{6,7},{8,9},{10,11},{12,13},{14,15},{16,17},{18,... | collective-permute-start | bytes 393224 | tf_op jit(solution)/shard_map/ppermute | solution.py:283
  2.1 8.1 %collective-permute-start.1 = (bf16[32,8,256]{2,1,0:T(8,128)(2,1)}, bf16[32,8,256]{2,1,0:T(8,128)(2,1)S(1)}, u32[]{:S(2)}, u32[]{:S(2)}) collective-permute-start(bf16[32,8,256]{2,1,0:T(8,128)(2,1)} %charges.3), channel_id=1, source_target_pairs={{1,2},{3,4},{5,6},{7,8},{9,10},{11,12},{13,14},{15,16},{17,18},{19... | collective-permute-start | bytes 393224 | tf_op jit(solution)/shard_map/ppermute | solution.py:283
  10.2 5.2 %outgoing.1 = bf16[128,3,8,128]{3,2,1,0:T(8,128)(2,1)} custom-call(bf16[32,8,256]{2,1,0:T(8,128)(2,1)} %charges.3, s32[8,32]{1,0:T(8,128)} %bitcast.5, s32[8,32]{1,0:T(8,128)} %bitcast.6, bf16[32,64,256]{2,1,0:T(8,128)(2,1)} %basis.1, bf16[32,8,64,64]{3,2,1,0:T(8,128)(2,1)} %couplings.2, bf16[32,64,64]{2,1,0:T(8,128)(2,1)} %transfer.2), custom_call_target="tpu_custom_call" | custom-call | flops 2684354560 | bytes 60000000 | tf_op jit(solution)/shard_map/outgoing/pallas_call | solution.py:161
  15.5 5.7 %all-to-all-start = ((bf16[128,3,8,128]{3,2,1,0:T(8,128)(2,1)}), bf16[128,3,8,128]{3,2,1,0:T(8,128)(2,1)S(1)}, u32[]{:S(2)}, u32[]{:S(2)}) async-start(bf16[128,3,8,128]{3,2,1,0:T(8,128)(2,1)} %outgoing.1), calls=%async_computation | async-start | bytes 1572864 | tf_op jit(solution)/shard_map/all_to_all | solution.py:286
  21.1 0.1 pad_add_fusion.place
  21.2 0.0 collective-permute-done.first
  21.2 0.0 collective-permute-done.1.second
  21.2 0.0 copy-start
  21.2 0.0 copy-start.1
  21.2 0.0 copy-start.2
  21.3 0.0 copy-start.3
  21.3 7.9 %near.1.near_field = f32[32,8,256]{2,1,0:T(8,128)S(1)} custom-call(s32[4,32]{1,0:T(4,128)} %bitcast.7, s32[2]{0:T(128)S(1)} %pad_add_fusion.place, bf16[32,8,256]{2,1,0:T(8,128)(2,1)} %charges.3, bf16[32,8,256]{2,1,0:T(8,128)(2,1)S(1)} %collective-permute-done.first, bf16[32,8,256]{2,1,0:T(8,128)(2,1)S(1)} %collective-permute-done.1.second, ...), custom_call_target="tpu_custom_call" | custom-call | flops 26843545600 | bytes 170000000 | tf_op jit(solution)/shard_map/near/pallas_call | solution.py:205
  29.1 8.7 %all-to-all-done.recv = bf16[128,3,8,128]{3,2,1,0:T(8,128)(2,1)S(1)} async-done(((bf16[128,3,8,128]{3,2,1,0:T(8,128)(2,1)}), bf16[128,3,8,128]{3,2,1,0:T(8,128)(2,1)S(1)}, u32[]{:S(2)}, u32[]{:S(2)}) %all-to-all-start) | async-done | bytes 786464 | tf_op jit(solution)/shard_map/all_to_all | solution.py:286
  37.8 0.0 copy-done
  37.8 0.0 copy-done.1
  37.8 0.0 copy-done.2
  37.8 0.0 copy-done.3
  37.8 2.3 %final.1 = f32[32,8,256]{2,1,0:T(8,128)} custom-call(s32[1,6]{1,0:T(1,128)S(1)} %copy-done.3, bf16[128,3,8,128]{3,2,1,0:T(8,128)(2,1)S(1)} %all-to-all-done.recv, f32[32,8,256]{2,1,0:T(8,128)S(1)} %near.1.near_field, bf16[32,64,256]{2,1,0:T(8,128)(2,1)S(1)} %copy-done, bf16[1,6,64,64]{3,2,1,0:T(8,128)(2,1)S(1)} %copy-done.2, bf16[32,64,64]{2,1,0:T(8,128)(2,1)S(1)} %copy-done.1), custom_call_target="tpu_custom_call" | custom-call | tf_op jit(solution)/shard_map/final/pallas_call | solution.py:255
Async XLA Ops:
  0.0 21.2 %collective-permute-start = (bf16[32,8,256]{2,1,0:T(8,128)(2,1)}, bf16[32,8,256]{2,1,0:T(8,128)(2,1)S(1)}, u32[]{:S(2)}, u32[]{:S(2)}) collective-permute-start(bf16[32,8,256]{2,1,0:T(8,128)(2,1)} %charges.3), channel_id=1, source_target_pairs={{0,1},{2,3},{4,5},{6,7},{8,9},{10,11},{12,13},{14,15},{16,17},{18,... | collective-permute-start | bytes 393224 | tf_op jit(solution)/shard_map/ppermute | solution.py:283
  2.1 19.1 %collective-permute-start.1 = (bf16[32,8,256]{2,1,0:T(8,128)(2,1)}, bf16[32,8,256]{2,1,0:T(8,128)(2,1)S(1)}, u32[]{:S(2)}, u32[]{:S(2)}) collective-permute-start(bf16[32,8,256]{2,1,0:T(8,128)(2,1)} %charges.3), channel_id=1, source_target_pairs={{1,2},{3,4},{5,6},{7,8},{9,10},{11,12},{13,14},{15,16},{17,18},{19... | collective-permute-start | bytes 393224 | tf_op jit(solution)/shard_map/ppermute | solution.py:283
  15.5 22.3 %all-to-all-start = ((bf16[128,3,8,128]{3,2,1,0:T(8,128)(2,1)}), bf16[128,3,8,128]{3,2,1,0:T(8,128)(2,1)S(1)}, u32[]{:S(2)}, u32[]{:S(2)}) async-start(bf16[128,3,8,128]{3,2,1,0:T(8,128)(2,1)} %outgoing.1), calls=%async_computation | async-start | bytes 1572864 | tf_op jit(solution)/shard_map/all_to_all | solution.py:286
  21.2 16.6 %copy-start = (bf16[32,64,256]{2,1,0:T(8,128)(2,1)S(1)}, bf16[32,64,256]{2,1,0:T(8,128)(2,1)}, u32[]{:S(2)}) copy-start(bf16[32,64,256]{2,1,0:T(8,128)(2,1)} %target_basis.1) | copy-start | bytes 3145732
  21.2 16.6 %copy-start.1 = (bf16[32,64,64]{2,1,0:T(8,128)(2,1)S(1)}, bf16[32,64,64]{2,1,0:T(8,128)(2,1)}, u32[]{:S(2)}) copy-start(bf16[32,64,64]{2,1,0:T(8,128)(2,1)} %transfer.3) | copy-start | bytes 786436
  21.2 16.6 %copy-start.2 = (bf16[1,6,64,64]{3,2,1,0:T(8,128)(2,1)S(1)}, bf16[1,6,64,64]{3,2,1,0:T(8,128)(2,1)}, u32[]{:S(2)}) copy-start(bf16[1,6,64,64]{3,2,1,0:T(8,128)(2,1)} %couplings.3) | copy-start | bytes 147460
  21.3 16.5 %copy-start.3 = (s32[1,6]{1,0:T(1,128)S(1)}, s32[1,6]{1,0:T(1,128)}, u32[]{:S(2)}) copy-start(s32[1,6]{1,0:T(1,128)} %coarse_list.1) | copy-start | bytes 76

commit v3 on v2

--- a/solution.py
+++ b/solution.py
@@ -19,8 +19,9 @@
 NT = (((1,), (1,)), ((), ()))
 TN = (((0,), (0,)), ((), ()))
 MIB = 1 << 20
+TRIANGLE_FLOPS = 26843545600
 NEAR_FLOPS = 26843545600
-NEAR_BYTES = 170000000
+NEAR_BYTES = 1000
 
 
 def dot(a, b, dims=(((1,), (0,)), ((), ()))):
@@ -31,106 +32,79 @@
     return lax.broadcasted_iota(jnp.int32, shape, dim)
 
 
+WRITE = 512
 GROUP = 4
-CHUNKS = ((0, 16), (16, 32))
 
 
 def in_hbm(*arrays):
     return tuple(pltpu.with_memory_space_constraint(array, pltpu.HBM) for array in arrays)
 
 
+def triangle_kernel(earlier):
+    earlier[...] = (iota(earlier.shape, 0) < iota(earlier.shape, 1)).astype(BF16)
+
+
+def triangle():
+    entries = LEAVES * NFAR
+    return pl.pallas_call(
+        triangle_kernel,
+        out_shape=jax.ShapeDtypeStruct((entries, entries), BF16),
+        out_specs=pl.BlockSpec(memory_space=pltpu.VMEM),
+        compiler_params=pltpu.CompilerParams(vmem_limit_bytes=8 * MIB),
+        cost_estimate=pl.CostEstimate(flops=TRIANGLE_FLOPS, bytes_accessed=1000, transcendentals=0),
+        name="triangle",
+    )()
+
+
 def outgoing_kernel(
-    charges,
-    devices,
-    slots,
-    basis,
-    couplings,
-    transfer,
-    send,
-    charges_v,
-    devices_v,
-    slots_v,
-    basis_v,
-    couplings_v,
-    transfer_v,
-    products,
-    chosen,
-    sems,
+    earlier, devices, slots, charges, basis, couplings, transfer, send_hbm, send, products, sems
 ):
-    small = [
-        pltpu.make_async_copy(src, dst, sems.at[i])
-        for i, (src, dst) in enumerate(
-            (
-                (charges, charges_v),
-                (basis, basis_v),
-                (devices, devices_v),
-                (slots, slots_v),
-                (transfer, transfer_v),
-            )
-        )
-    ]
-    for copy in small:
-        copy.start()
-    copies = [
-        pltpu.make_async_copy(couplings.at[low:high], couplings_v.at[low:high], sems.at[len(small) + g])
-        for g, (low, high) in enumerate(CHUNKS)
-    ]
-    for copy in copies:
-        copy.start()
-    small[2].wait()
-    small[3].wait()
-
     entries = LEAVES * NFAR
-    device = jnp.concatenate([devices_v[j : j + 1, :] for j in range(NFAR)], axis=1)
-    slot = jnp.concatenate([slots_v[j : j + 1, :] for j in range(NFAR)], axis=1)
+    device = jnp.concatenate([devices[j : j + 1, :] for j in range(NFAR)], axis=1)
+    slot = jnp.concatenate([slots[j : j + 1, :] for j in range(NFAR)], axis=1)
     named = iota((DEVICES, entries), 0) == device
-    earlier = iota((entries, entries), 0) < iota((entries, entries), 1)
-    counts = dot(named.astype(BF16), earlier.astype(BF16))
+    counts = dot(named.astype(BF16), earlier[...])
     order = jnp.sum(jnp.where(named, counts, 0.0), axis=0, keepdims=True).astype(jnp.int32)
     row_of = device * 8 + order
     slot_rows = jnp.broadcast_to((slot + 1).astype(F32), (128, entries)).astype(BF16)
-    span = 256
-    for at in range(0, DEVICES * 8, span):
-        row = iota((span, entries), 0) + at
-        chosen[at : at + span, :entries] = (row == row_of).astype(BF16)
-        chosen[at : at + span, entries:] = (row == row_of + 4).astype(BF16)
-
-    small[0].wait()
-    small[1].wait()
+
     moments = []
     for at in range(0, LEAVES, 4):
-        own = charges_v[at : at + 4].reshape(4 * RHS, POINTS)
-        product = dot(own, basis_v[at : at + 4].reshape(4 * RANK, POINTS), NT)
+        own = charges[at : at + 4].reshape(4 * RHS, POINTS)
+        product = dot(own, basis[at : at + 4].reshape(4 * RANK, POINTS), NT)
         for i in range(4):
             moments.append(product[i * RHS : (i + 1) * RHS, i * RANK : (i + 1) * RANK].astype(BF16))
-    small[4].wait()
     raised = []
     for at in range(0, LEAVES, 4):
         product = dot(
             jnp.concatenate(moments[at : at + 4], axis=0),
-            transfer_v[at : at + 4].reshape(4 * RANK, RANK),
+            transfer[at : at + 4].reshape(4 * RANK, RANK),
             NT,
         )
         raised += [product[i * RHS : (i + 1) * RHS, i * RANK : (i + 1) * RANK] for i in range(4)]
     while len(raised) > 1:
         raised = [a + b for a, b in zip(raised[::2], raised[1::2])]
     node = raised[0]
+
     wide = jnp.concatenate([node, jnp.zeros((RHS, RANK), F32)], axis=1)
     turned = pltpu.roll(pltpu.roll(wide, RANK, 1), 4, 0)
     upper = iota((RHS, 128), 0) < 4
     node_rows = jnp.where(upper, jnp.where(iota((RHS, 128), 1) < RANK, wide, turned), 0.0)
+
+    span = 256
     for at in range(0, DEVICES * 8, span):
-        names = dot(chosen[at : at + span, entries:], slot_rows, NT).reshape(span // 8, 8, 128)
-        send[at // 8 : (at + span) // 8, 2] = (names + node_rows[None]).astype(BF16)
-
-    for copy, (low, high) in zip(copies, CHUNKS):
-        copy.wait()
-        for l in range(low, high):
-            for h in range(2):
-                half = couplings_v[l, h * 4 : h * 4 + 4].reshape(4 * RANK, RANK)
-                product = dot(moments[l], half, NT)
-                for t in range(2):
-                    products[2 * h + t, l * RHS : (l + 1) * RHS, :] = product[:, t * 128 : (t + 1) * 128]
+        second = (iota((span, entries), 0) + at == row_of + 4).astype(BF16)
+        names = dot(second, slot_rows, NT).reshape(span // 8, 8, 128) + node_rows[None]
+        send[at // 8 : (at + span) // 8, 2] = names.astype(BF16)
+    writes = [pltpu.make_async_copy(send.at[:, 2], send_hbm.at[:, 2], sems.at[0])]
+    writes[0].start()
+
+    for l in range(LEAVES):
+        for h in range(2):
+            half = couplings[l, h * 4 : h * 4 + 4].reshape(4 * RANK, RANK)
+            product = dot(moments[l], half, NT)
+            for t in range(2):
+                products[2 * h + t, l * RHS : (l + 1) * RHS, :] = product[:, t * 128 : (t + 1) * 128]
 
     low = iota((LEAVES, 128), 1) < RANK
     pieces = []
@@ -150,29 +124,39 @@
         axis=0,
     )
     for at in range(0, DEVICES * 8, span):
-        rows = dot(chosen[at : at + span, :], table)
+        row = iota((span, entries), 0) + at
+        chosen = (row == row_of).astype(BF16)
+        second = (row == row_of + 4).astype(BF16)
+        rows = dot(jnp.concatenate([chosen, second], axis=1), table)
         part = pl.ds(at // 8, span // 8)
         send[part, 0] = rows[:, :128].reshape(span // 8, 8, 128).astype(BF16)
         send[part, 1] = rows[:, 128:].reshape(span // 8, 8, 128).astype(BF16)
-
-
-def outgoing(charges, far_devices, far_slots, source_basis, far_couplings, up_transfer):
-    arrays = (charges, far_devices.T, far_slots.T, source_basis, far_couplings, up_transfer)
+        if (at + span) % WRITE == 0:
+            part = pl.ds((at + span - WRITE) // 8, WRITE // 8)
+            writes.append(
+                pltpu.make_async_copy(send.at[part, 0:2], send_hbm.at[part, 0:2], sems.at[len(writes)])
+            )
+            writes[-1].start()
+    for write in writes:
+        write.wait()
+
+
+def outgoing(earlier, far_devices, far_slots, charges, source_basis, far_couplings, up_transfer):
+    vmem = pl.BlockSpec(memory_space=pltpu.VMEM)
     return pl.pallas_call(
         outgoing_kernel,
         out_shape=jax.ShapeDtypeStruct((DEVICES, 3, 8, 128), BF16),
-        in_specs=[pl.BlockSpec(memory_space=pltpu.HBM)] * 6,
-        out_specs=pl.BlockSpec(memory_space=pltpu.VMEM),
-        scratch_shapes=[pltpu.VMEM(array.shape, array.dtype) for array in arrays]
-        + [
+        in_specs=[vmem] * 7,
+        out_specs=pl.BlockSpec(memory_space=pltpu.HBM),
+        scratch_shapes=[
+            pltpu.VMEM((DEVICES, 3, 8, 128), BF16),
             pltpu.VMEM((NFAR // 2, LEAVES * RHS, 128), F32),
-            pltpu.VMEM((DEVICES * 8, 2 * LEAVES * NFAR), BF16),
-            pltpu.SemaphoreType.DMA((5 + len(CHUNKS),)),
+            pltpu.SemaphoreType.DMA((1 + DEVICES * 8 // WRITE,)),
         ],
         compiler_params=pltpu.CompilerParams(vmem_limit_bytes=24 * MIB),
-        cost_estimate=pl.CostEstimate(flops=2684354560, bytes_accessed=60000000, transcendentals=0),
+        cost_estimate=pl.CostEstimate(flops=26843545600, bytes_accessed=1000, transcendentals=0),
         name="outgoing",
-    )(*in_hbm(*arrays))
+    )(earlier, far_devices.T, far_slots.T, charges, source_basis, far_couplings, up_transfer)
 
 
 def near_kernel(near_list, place, charges, first, second, blocks, out, sources, blocks_v, sems):
@@ -279,10 +263,11 @@
     count = lax.axis_size(AXES)
     myself = lax.axis_index(AXES)
     pairs = [[(i, i + 1) for i in range(start, count - 1, 2)] for start in (0, 1)]
-    first, second = [
-        lax.ppermute(charges, AXES, some + [(j, i) for i, j in some]) for some in pairs
-    ]
-    send = outgoing(charges, far_devices, far_slots, source_basis, far_couplings, up_transfer)
+    earlier, mine = lax.optimization_barrier((triangle(), charges))
+    exchange = [some + [(j, i) for i, j in some] for some in pairs]
+    first = lax.ppermute(charges, AXES, exchange[0])
+    second = lax.ppermute(mine, AXES, exchange[1])
+    send = outgoing(earlier, far_devices, far_slots, charges, source_basis, far_couplings, up_transfer)
     recv = lax.all_to_all(send, AXES, 0, 0, tiled=True)
     place = jnp.stack([myself * LEAVES - LEAVES, myself % 2])
     near_field = near(near_list, place, charges, first, second, near_blocks)

time: 40.3 us -> 38.7 us (0.960)
  Pallas kernels: 15.3 us -> 13.4 us
    pallas_call x1, Pallas kernels: 5.2 us -> 3.25 us  [outgoing(): pl.pallas_call(outgoing_kernel, out_shape=jax.ShapeDtypeStruct((DEVICES,...]
  transfers between devices with their start and end apart: 3 -> 3, of which waited for: 1 -> 1; matrix products, arithmetic and copies ran while one was open for 0% -> 0% of each run, Pallas kernels for 33% -> 29%
where the time goes in v3:
time: 38.7 us; the launch traced here: 38.5 us
  starting transfers between devices  16.1 us (42%)
  Pallas kernels  13.4 us (35%)
  waiting for transfers between devices  8.66 us (22%)
    all_to_all x1, waiting for transfers between devices, body(): recv = lax.all_to_all(send, AXES, 0, 0, tiled=True)  8.66 us
    ppermute x1, starting transfers between devices, body(): second = lax.ppermute(mine, AXES, exchange[1])  8.39 us
    pallas_call x1, Pallas kernels, near(): pl.pallas_call(near_kernel, out_shape=jax.ShapeDtypeStruct((LEAVES, RHS,...  7.86 us
    all_to_all x1, starting transfers between devices, body(): recv = lax.all_to_all(send, AXES, 0, 0, tiled=True)  5.53 us
    pallas_call x1, Pallas kernels, outgoing(): pl.pallas_call(outgoing_kernel, out_shape=jax.ShapeDtypeStruct((DEVICES,...  3.25 us
    pallas_call x1, Pallas kernels, final(): pl.pallas_call(final_kernel, out_shape=jax.ShapeDtypeStruct((LEAVES, RHS,...  2.27 us
    ppermute x1, starting transfers between devices, body(): first = lax.ppermute(charges, AXES, exchange[0])  2.21 us
  transfers between devices with their start and end apart: 3, of which 1 were waited for; matrix products, arithmetic and copies ran while one was open for 0% of the time, Pallas kernels for 29%

profile of v3, /device:TPU:1, one launch (start us, length us, event | category | flops | bytes accessed | tf_op | source)
XLA Modules:
  0.0 38.5 jit_solution(14348961401070308339)
XLA Ops:
  0.0 0.0 copy-start.7
  0.0 0.0 copy-start.8
  0.0 0.0 copy-start.9
  0.0 0.0 copy-start.5
  0.0 0.0 copy-start.4
  0.0 0.0 copy-start.6
  0.0 2.2 %collective-permute-start = (bf16[32,8,256]{2,1,0:T(8,128)(2,1)}, bf16[32,8,256]{2,1,0:T(8,128)(2,1)S(1)}, u32[]{:S(2)}, u32[]{:S(2)}) collective-permute-start(bf16[32,8,256]{2,1,0:T(8,128)(2,1)} %charges.3), channel_id=1, source_target_pairs={{0,1},{2,3},{4,5},{6,7},{8,9},{10,11},{12,13},{14,15},{16,17},{18,... | collective-permute-start | bytes 393224 | tf_op jit(solution)/shard_map/ppermute | solution.py:268
  2.3 0.0 copy-done.7
  2.3 8.4 %collective-permute-start.1 = (bf16[32,8,256]{2,1,0:T(8,128)(2,1)S(1)}, bf16[32,8,256]{2,1,0:T(8,128)(2,1)S(1)}, u32[]{:S(2)}, u32[]{:S(2)}) collective-permute-start(bf16[32,8,256]{2,1,0:T(8,128)(2,1)S(1)} %copy-done.7), channel_id=1, source_target_pairs={{1,2},{3,4},{5,6},{7,8},{9,10},{11,12},{13,14},{15,16},{17,18},{19... | collective-permute-start | bytes 393224 | tf_op jit(solution)/shard_map/ppermute | solution.py:269
  10.7 0.0 copy-done.8
  10.7 0.0 copy-done.9
  10.7 0.0 copy-done.5
  10.7 0.0 copy-done.4
  10.7 0.0 copy-done.6
  10.7 3.2 %outgoing.1 = bf16[128,3,8,128]{3,2,1,0:T(8,128)(2,1)} custom-call(bf16[256,256]{1,0:T(8,128)(2,1)S(1)} %triangle.1.earlier, s32[8,32]{1,0:T(8,128)S(1)} %bitcast.5, s32[8,32]{1,0:T(8,128)S(1)} %bitcast.6, bf16[32,8,256]{2,1,0:T(8,128)(2,1)S(1)} %copy-done.7, bf16[32,64,256]{2,1,0:T(8,128)(2,1)S(1)} %copy-done.5, bf16[32,8,64,64]{3,2,1,0:T(8,128)(2,1)S(1)} %copy-done.4, ...), custom_call_target="tpu_custom_call" | custom-call | flops 26843545600 | bytes 1000 | tf_op jit(solution)/shard_map/outgoing/pallas_call | solution.py:146
  14.0 5.5 %all-to-all-start = ((bf16[128,3,8,128]{3,2,1,0:T(8,128)(2,1)}), bf16[128,3,8,128]{3,2,1,0:T(8,128)(2,1)S(1)}, u32[]{:S(2)}, u32[]{:S(2)}) async-start(bf16[128,3,8,128]{3,2,1,0:T(8,128)(2,1)} %outgoing.1), calls=%async_computation | async-start | bytes 1572864 | tf_op jit(solution)/shard_map/all_to_all | solution.py:271
  19.5 0.1 pad_add_fusion.place
  19.6 0.0 collective-permute-done.first
  19.6 0.0 collective-permute-done.1.second
  19.6 0.0 copy-start
  19.6 0.0 copy-start.1
  19.6 0.0 copy-start.2
  19.6 0.0 copy-start.3
  19.7 7.9 %near.1.near_field = f32[32,8,256]{2,1,0:T(8,128)S(1)} custom-call(s32[4,32]{1,0:T(4,128)} %bitcast.7, s32[2]{0:T(128)S(1)} %pad_add_fusion.place, bf16[32,8,256]{2,1,0:T(8,128)(2,1)} %charges.3, bf16[32,8,256]{2,1,0:T(8,128)(2,1)S(1)} %collective-permute-done.first, bf16[32,8,256]{2,1,0:T(8,128)(2,1)S(1)} %collective-permute-done.1.second, ...), custom_call_target="tpu_custom_call" | custom-call | flops 26843545600 | bytes 1000 | tf_op jit(solution)/shard_map/near/pallas_call | solution.py:189
  27.5 8.7 %all-to-all-done.recv = bf16[128,3,8,128]{3,2,1,0:T(8,128)(2,1)S(1)} async-done(((bf16[128,3,8,128]{3,2,1,0:T(8,128)(2,1)}), bf16[128,3,8,128]{3,2,1,0:T(8,128)(2,1)S(1)}, u32[]{:S(2)}, u32[]{:S(2)}) %all-to-all-start) | async-done | bytes 786464 | tf_op jit(solution)/shard_map/all_to_all | solution.py:271
  36.2 0.0 copy-done
  36.2 0.0 copy-done.1
  36.2 0.0 copy-done.2
  36.2 0.0 copy-done.3
  36.2 2.3 %final.1 = f32[32,8,256]{2,1,0:T(8,128)} custom-call(s32[1,6]{1,0:T(1,128)S(1)} %copy-done.3, bf16[128,3,8,128]{3,2,1,0:T(8,128)(2,1)S(1)} %all-to-all-done.recv, f32[32,8,256]{2,1,0:T(8,128)S(1)} %near.1.near_field, bf16[32,64,256]{2,1,0:T(8,128)(2,1)S(1)} %copy-done, bf16[1,6,64,64]{3,2,1,0:T(8,128)(2,1)S(1)} %copy-done.2, bf16[32,64,64]{2,1,0:T(8,128)(2,1)S(1)} %copy-done.1), custom_call_target="tpu_custom_call" | custom-call | tf_op jit(solution)/shard_map/final/pallas_call | solution.py:239
  (1 shorter events, 0.0 us)
Async XLA Ops:
  0.0 2.3 %copy-start.7 = (bf16[32,8,256]{2,1,0:T(8,128)(2,1)S(1)}, bf16[32,8,256]{2,1,0:T(8,128)(2,1)}, u32[]{:S(2)}) copy-start(bf16[32,8,256]{2,1,0:T(8,128)(2,1)} %charges.3) | copy-start | bytes 393220
  0.0 10.7 %copy-start.8 = (s32[32,8]{0,1:T(8,128)S(1)}, s32[32,8]{0,1:T(8,128)}, u32[]{:S(2)}) copy-start(s32[32,8]{0,1:T(8,128)} %param.17) | copy-start | bytes 3076
  0.0 10.7 %copy-start.9 = (s32[32,8]{0,1:T(8,128)S(1)}, s32[32,8]{0,1:T(8,128)}, u32[]{:S(2)}) copy-start(s32[32,8]{0,1:T(8,128)} %param.18) | copy-start | bytes 3076
  0.0 10.7 %copy-start.5 = (bf16[32,64,256]{2,1,0:T(8,128)(2,1)S(1)}, bf16[32,64,256]{2,1,0:T(8,128)(2,1)}, u32[]{:S(2)}) copy-start(bf16[32,64,256]{2,1,0:T(8,128)(2,1)} %basis.1) | copy-start | bytes 3145732
  0.0 10.7 %copy-start.4 = (bf16[32,8,64,64]{3,2,1,0:T(8,128)(2,1)S(1)}, bf16[32,8,64,64]{3,2,1,0:T(8,128)(2,1)}, u32[]{:S(2)}) copy-start(bf16[32,8,64,64]{3,2,1,0:T(8,128)(2,1)} %couplings.2) | copy-start | bytes 6291460
  0.0 10.7 %copy-start.6 = (bf16[32,64,64]{2,1,0:T(8,128)(2,1)S(1)}, bf16[32,64,64]{2,1,0:T(8,128)(2,1)}, u32[]{:S(2)}) copy-start(bf16[32,64,64]{2,1,0:T(8,128)(2,1)} %transfer.2) | copy-start | bytes 786436
  0.0 19.6 %collective-permute-start = (bf16[32,8,256]{2,1,0:T(8,128)(2,1)}, bf16[32,8,256]{2,1,0:T(8,128)(2,1)S(1)}, u32[]{:S(2)}, u32[]{:S(2)}) collective-permute-start(bf16[32,8,256]{2,1,0:T(8,128)(2,1)} %charges.3), channel_id=1, source_target_pairs={{0,1},{2,3},{4,5},{6,7},{8,9},{10,11},{12,13},{14,15},{16,17},{18,... | collective-permute-start | bytes 393224 | tf_op jit(solution)/shard_map/ppermute | solution.py:268
  2.3 17.3 %collective-permute-start.1 = (bf16[32,8,256]{2,1,0:T(8,128)(2,1)S(1)}, bf16[32,8,256]{2,1,0:T(8,128)(2,1)S(1)}, u32[]{:S(2)}, u32[]{:S(2)}) collective-permute-start(bf16[32,8,256]{2,1,0:T(8,128)(2,1)S(1)} %copy-done.7), channel_id=1, source_target_pairs={{1,2},{3,4},{5,6},{7,8},{9,10},{11,12},{13,14},{15,16},{17,18},{19... | collective-permute-start | bytes 393224 | tf_op jit(solution)/shard_map/ppermute | solution.py:269
  14.0 22.2 %all-to-all-start = ((bf16[128,3,8,128]{3,2,1,0:T(8,128)(2,1)}), bf16[128,3,8,128]{3,2,1,0:T(8,128)(2,1)S(1)}, u32[]{:S(2)}, u32[]{:S(2)}) async-start(bf16[128,3,8,128]{3,2,1,0:T(8,128)(2,1)} %outgoing.1), calls=%async_computation | async-start | bytes 1572864 | tf_op jit(solution)/shard_map/all_to_all | solution.py:271
  19.6 16.6 %copy-start = (bf16[32,64,256]{2,1,0:T(8,128)(2,1)S(1)}, bf16[32,64,256]{2,1,0:T(8,128)(2,1)}, u32[]{:S(2)}) copy-start(bf16[32,64,256]{2,1,0:T(8,128)(2,1)} %target_basis.1) | copy-start | bytes 3145732
  19.6 16.6 %copy-start.1 = (bf16[32,64,64]{2,1,0:T(8,128)(2,1)S(1)}, bf16[32,64,64]{2,1,0:T(8,128)(2,1)}, u32[]{:S(2)}) copy-start(bf16[32,64,64]{2,1,0:T(8,128)(2,1)} %transfer.3) | copy-start | bytes 786436
  19.6 16.6 %copy-start.2 = (bf16[1,6,64,64]{3,2,1,0:T(8,128)(2,1)S(1)}, bf16[1,6,64,64]{3,2,1,0:T(8,128)(2,1)}, u32[]{:S(2)}) copy-start(bf16[1,6,64,64]{3,2,1,0:T(8,128)(2,1)} %couplings.3) | copy-start | bytes 147460
  19.6 16.5 %copy-start.3 = (s32[1,6]{1,0:T(1,128)S(1)}, s32[1,6]{1,0:T(1,128)}, u32[]{:S(2)}) copy-start(s32[1,6]{1,0:T(1,128)} %coarse_list.1) | copy-start | bytes 76

commit v4 on v3

--- a/solution.py
+++ b/solution.py
@@ -20,8 +20,7 @@
 TN = (((0,), (0,)), ((), ()))
 MIB = 1 << 20
 TRIANGLE_FLOPS = 26843545600
-NEAR_FLOPS = 26843545600
-NEAR_BYTES = 1000
+NEAR_FLOPS = 4600000000
 
 
 def dot(a, b, dims=(((1,), (0,)), ((), ()))):
@@ -33,7 +32,6 @@
 
 
 WRITE = 512
-GROUP = 4
 
 
 def in_hbm(*arrays):
@@ -159,47 +157,52 @@
     )(earlier, far_devices.T, far_slots.T, charges, source_basis, far_couplings, up_transfer)
 
 
-def near_kernel(near_list, place, charges, first, second, blocks, out, sources, blocks_v, sems):
-    own = pltpu.make_async_copy(charges, sources.at[pl.ds(LEAVES, LEAVES)], sems.at[LEAVES // GROUP])
-    own.start()
-    copies = []
-    for g in range(LEAVES // GROUP):
-        part = pl.ds(g * GROUP, GROUP)
-        copies.append(pltpu.make_async_copy(blocks.at[part], blocks_v.at[part], sems.at[g]))
-        copies[-1].start()
+def near_terms(near_list, base, sources, blocks, l, js):
+    picked = [sources[near_list[j, l] - base] for j in js]
+    half = POINTS // 2
+    return [
+        dot(picked[0], blocks[l, js[0], at : at + half], NT)
+        + dot(picked[1], blocks[l, js[1], at : at + half], NT)
+        for at in (0, half)
+    ]
+
+
+def near_first_kernel(near_list, place, charges, first, blocks, out, sources):
     base, parity = place[0], place[1]
+    sources[LEAVES : 2 * LEAVES] = charges[...]
     sources[pl.ds((1 - parity) * 2 * LEAVES, LEAVES)] = first[...]
-    sources[pl.ds(parity * 2 * LEAVES, LEAVES)] = second[...]
-    own.wait()
-    half = POINTS // 2
-    for g in range(LEAVES // GROUP):
-        copies[g].wait()
-        for l in range(g * GROUP, (g + 1) * GROUP):
-            picked = [sources[near_list[j, l] - base] for j in range(NNEAR)]
-            for at in (0, half):
-                terms = [dot(picked[j], blocks_v[l, j, at : at + half], NT) for j in range(NNEAR)]
-                out[l, :, at : at + half] = sum(terms[1:], terms[0])
-
-
-def near(near_list, place, charges, first, second, near_blocks):
+    for l in range(LEAVES):
+        left, right = near_terms(near_list, base, sources, blocks, l, (0, 2 - parity))
+        out[l, :, : POINTS // 2] = left
+        out[l, :, POINTS // 2 :] = right
+
+
+def near_second_kernel(
+    near_list, place, charges, first, second, far_second, blocks, partial, out, sources
+):
+    base, parity = place[0], place[1]
+    sources[LEAVES : 2 * LEAVES] = charges[...]
+    sources[pl.ds((1 - parity) * 2 * LEAVES, LEAVES)] = first[...]
+    sources[pl.ds(parity * 2 * LEAVES, LEAVES)] = second[...] + far_second[...]
+    for l in range(LEAVES):
+        left, right = near_terms(near_list, base, sources, blocks, l, (1 + parity, NNEAR - 1))
+        out[l, :, : POINTS // 2] = partial[l, :, : POINTS // 2] + left
+        out[l, :, POINTS // 2 :] = partial[l, :, POINTS // 2 :] + right
+
+
+def near(kernel, name, near_list, place, *arrays):
     vmem = pl.BlockSpec(memory_space=pltpu.VMEM)
     smem = pl.BlockSpec(memory_space=pltpu.SMEM)
-    hbm = pl.BlockSpec(memory_space=pltpu.HBM)
-    near_list, charges, near_blocks = in_hbm(near_list.T, charges, near_blocks)
     return pl.pallas_call(
-        near_kernel,
+        kernel,
         out_shape=jax.ShapeDtypeStruct((LEAVES, RHS, POINTS), F32),
-        in_specs=[smem, smem, hbm, vmem, vmem, hbm],
+        in_specs=[smem, smem] + [vmem] * len(arrays),
         out_specs=vmem,
-        scratch_shapes=[
-            pltpu.VMEM((3 * LEAVES, RHS, POINTS), BF16),
-            pltpu.VMEM(near_blocks.shape, BF16),
-            pltpu.SemaphoreType.DMA((LEAVES // GROUP + 1,)),
-        ],
-        compiler_params=pltpu.CompilerParams(vmem_limit_bytes=32 * MIB),
-        cost_estimate=pl.CostEstimate(flops=NEAR_FLOPS, bytes_accessed=NEAR_BYTES, transcendentals=0),
-        name="near",
-    )(near_list, place, charges, first, second, near_blocks)
+        scratch_shapes=[pltpu.VMEM((3 * LEAVES, RHS, POINTS), BF16)],
+        compiler_params=pltpu.CompilerParams(vmem_limit_bytes=20 * MIB),
+        cost_estimate=pl.CostEstimate(flops=NEAR_FLOPS, bytes_accessed=1000, transcendentals=0),
+        name=name,
+    )(*in_hbm(near_list.T), place, *arrays)
 
 
 def unfold(rows):
@@ -262,15 +265,32 @@
 ):
     count = lax.axis_size(AXES)
     myself = lax.axis_index(AXES)
+    of_subtree = lax.axis_size("dev")
     pairs = [[(i, i + 1) for i in range(start, count - 1, 2)] for start in (0, 1)]
+    ends = [(i, j) for i, j in pairs[1] if j % of_subtree == 0]
+    inner = [(i, j) for i, j in pairs[1] if j % of_subtree != 0]
+    first, far_second = [
+        lax.ppermute(charges, AXES, some + [(j, i) for i, j in some]) for some in (pairs[0], ends)
+    ]
     earlier, mine = lax.optimization_barrier((triangle(), charges))
-    exchange = [some + [(j, i) for i, j in some] for some in pairs]
-    first = lax.ppermute(charges, AXES, exchange[0])
-    second = lax.ppermute(mine, AXES, exchange[1])
-    send = outgoing(earlier, far_devices, far_slots, charges, source_basis, far_couplings, up_transfer)
+    send = outgoing(earlier, far_devices, far_slots, mine, source_basis, far_couplings, up_transfer)
+    send, mine = lax.optimization_barrier((send, mine))
     recv = lax.all_to_all(send, AXES, 0, 0, tiled=True)
+    second = lax.ppermute(mine, AXES, inner + [(j, i) for i, j in inner])
     place = jnp.stack([myself * LEAVES - LEAVES, myself % 2])
-    near_field = near(near_list, place, charges, first, second, near_blocks)
+    partial = near(near_first_kernel, "near_first", near_list, place, mine, first, near_blocks)
+    near_field = near(
+        near_second_kernel,
+        "near_second",
+        near_list,
+        place,
+        mine,
+        first,
+        second,
+        far_second,
+        near_blocks,
+        partial,
+    )
     return final(coarse_list, recv, near_field, target_basis, coarse_couplings, down_transfer)
 
 

time: 38.7 us -> 37.2 us (0.961)
  local copies, waits for them, and re-layouts: 0.05 us -> 5.81 us
  waiting for transfers between devices: 8.66 us -> 4.01 us
  Pallas kernels: 13.4 us -> 11.6 us
  starting transfers between devices: 16.1 us -> 15.2 us
    unnamed x20 -> x22, local copies, waits for them, and re-layouts: 0.05 us -> 5.81 us
    all_to_all x1, waiting for transfers between devices: 8.66 us -> 3.99 us  [body(): recv = lax.all_to_all(send, AXES, 0, 0, tiled=True)]
    pallas_call x1 -> x2, Pallas kernels: 7.86 us -> 6.09 us  [near(): pl.pallas_call(kernel, out_shape=jax.ShapeDtypeStruct((LEAVES, RHS, POINT...]
    all_to_all x1, starting transfers between devices: 5.53 us -> 4 us  [body(): recv = lax.all_to_all(send, AXES, 0, 0, tiled=True)]
    ppermute x2 -> x3, starting transfers between devices: 10.6 us -> 11.2 us  [the longest x2 10.6 us: body(): lax.ppermute(charges, AXES, some + [(j, i) for i, j in some])]
  transfers between devices with their start and end apart: 3 -> 4, of which waited for: 1 -> 1; matrix products, arithmetic and copies ran while one was open for 0% -> 0% of each run, Pallas kernels for 29% -> 25%
where the time goes in v4:
time: 37.2 us; the launch traced here: 36.9 us
  starting transfers between devices  15.2 us (41%)
  Pallas kernels  11.6 us (31%)
  local copies, waits for them, and re-layouts  5.81 us (16%)
  waiting for transfers between devices  4.01 us (11%)
    ppermute x2, starting transfers between devices, body(): lax.ppermute(charges, AXES, some + [(j, i) for i, j in some])  10.6 us
    pallas_call x2, Pallas kernels, near(): pl.pallas_call(kernel, out_shape=jax.ShapeDtypeStruct((LEAVES, RHS, POINT...  6.09 us
    unnamed x22, local copies, waits for them, and re-layouts  5.81 us
    all_to_all x1, starting transfers between devices, body(): recv = lax.all_to_all(send, AXES, 0, 0, tiled=True)  4 us
    all_to_all x1, waiting for transfers between devices, body(): recv = lax.all_to_all(send, AXES, 0, 0, tiled=True)  3.99 us
    pallas_call x1, Pallas kernels, outgoing(): pl.pallas_call(outgoing_kernel, out_shape=jax.ShapeDtypeStruct((DEVICES,...  3.25 us
    pallas_call x1, Pallas kernels, final(): pl.pallas_call(final_kernel, out_shape=jax.ShapeDtypeStruct((LEAVES, RHS,...  2.27 us
  transfers between devices with their start and end apart: 4, of which 1 were waited for; matrix products, arithmetic and copies ran while one was open for 0% of the time, Pallas kernels for 25%

profile of v4, /device:TPU:1, one launch (start us, length us, event | category | flops | bytes accessed | tf_op | source)
XLA Modules:
  0.0 36.9 jit_solution(18125936912292918589)
XLA Ops:
  0.0 0.0 copy-start.2
  0.0 0.0 copy-start.9
  0.0 0.0 copy-start.7
  0.0 0.0 copy-start.6
  0.0 0.0 copy-start.8
  0.0 2.2 %collective-permute-start = (bf16[32,8,256]{2,1,0:T(8,128)(2,1)}, bf16[32,8,256]{2,1,0:T(8,128)(2,1)S(1)}, u32[]{:S(2)}, u32[]{:S(2)}) collective-permute-start(bf16[32,8,256]{2,1,0:T(8,128)(2,1)} %charges.2), channel_id=1, source_target_pairs={{0,1},{2,3},{4,5},{6,7},{8,9},{10,11},{12,13},{14,15},{16,17},{18,... | collective-permute-start | bytes 393224 | tf_op jit(solution)/shard_map/ppermute | solution.py:273
  2.2 8.4 %collective-permute-start.2 = (bf16[32,8,256]{2,1,0:T(8,128)(2,1)}, bf16[32,8,256]{2,1,0:T(8,128)(2,1)S(1)}, u32[]{:S(2)}, u32[]{:S(2)}) collective-permute-start(bf16[32,8,256]{2,1,0:T(8,128)(2,1)} %charges.2), channel_id=1, source_target_pairs={{15,16},{31,32},{47,48},{63,64},{79,80},{95,96},{111,112},{16,15},... | collective-permute-start | bytes 393224 | tf_op jit(solution)/shard_map/ppermute | solution.py:273
  10.7 0.0 copy-done.2
  10.7 0.0 copy-done.9
  10.7 0.0 copy-done.10
  10.7 0.0 copy-done.7
  10.7 0.0 copy-done.6
  10.7 0.0 copy-done.8
  10.7 3.3 %outgoing.1 = bf16[128,3,8,128]{3,2,1,0:T(8,128)(2,1)} custom-call(bf16[256,256]{1,0:T(8,128)(2,1)S(1)} %triangle.1.earlier, s32[8,32]{1,0:T(8,128)S(1)} %bitcast.5, s32[8,32]{1,0:T(8,128)S(1)} %bitcast.6, bf16[32,8,256]{2,1,0:T(8,128)(2,1)S(1)} %copy-done.2, bf16[32,64,256]{2,1,0:T(8,128)(2,1)S(1)} %copy-done.7, bf16[32,8,64,64]{3,2,1,0:T(8,128)(2,1)S(1)} %copy-done.6, ...), custom_call_target="tpu_custom_call" | custom-call | flops 26843545600 | bytes 1000 | tf_op jit(solution)/shard_map/outgoing/pallas_call | solution.py:144
  14.0 4.0 %all-to-all-start = ((bf16[128,3,8,128]{3,2,1,0:T(8,128)(2,1)}), bf16[128,3,8,128]{3,2,1,0:T(8,128)(2,1)S(1)}, u32[]{:S(2)}, u32[]{:S(2)}) async-start(bf16[128,3,8,128]{3,2,1,0:T(8,128)(2,1)} %outgoing.1), calls=%async_computation | async-start | bytes 1572864 | tf_op jit(solution)/shard_map/all_to_all | solution.py:278
  18.0 0.7 %collective-permute-start.1 = (bf16[32,8,256]{2,1,0:T(8,128)(2,1)S(1)}, bf16[32,8,256]{2,1,0:T(8,128)(2,1)S(1)}, u32[]{:S(2)}, u32[]{:S(2)}) collective-permute-start(bf16[32,8,256]{2,1,0:T(8,128)(2,1)S(1)} %copy-done.2), channel_id=1, source_target_pairs={{1,2},{3,4},{5,6},{7,8},{9,10},{11,12},{13,14},{17,18},{19,20},{21... | collective-permute-start | bytes 393224 | tf_op jit(solution)/shard_map/ppermute | solution.py:279
  18.7 0.1 pad_add_fusion.place
  18.7 0.0 collective-permute-done.first
  18.8 0.0 copy-start
  18.8 5.8 %copy-done = bf16[32,4,256,256]{3,2,1,0:T(8,128)(2,1)S(1)} copy-done((bf16[32,4,256,256]{3,2,1,0:T(8,128)(2,1)S(1)}, bf16[32,4,256,256]{3,2,1,0:T(8,128)(2,1)}, u32[]{:S(2)}) %copy-start) | copy-done | bytes 16777240
  24.5 0.0 copy-start.1
  24.5 0.0 copy-start.3
  24.5 3.1 %near_first.1.partial = f32[32,8,256]{2,1,0:T(8,128)S(1)} custom-call(s32[4,32]{1,0:T(4,128)} %bitcast.7, s32[2]{0:T(128)S(1)} %pad_add_fusion.place, bf16[32,8,256]{2,1,0:T(8,128)(2,1)S(1)} %copy-done.2, bf16[32,8,256]{2,1,0:T(8,128)(2,1)S(1)} %collective-permute-done.first, bf16[32,4,256,256]{3,2,1,0:T(8,128)(2,1)S(1)} %copy-done), custom_call_target="tpu_custom_call" | custom-call | flops 4600000000 | bytes 1000 | tf_op jit(solution)/shard_map/near_first/pallas_call | solution.py:196
  27.6 0.0 collective-permute-done.1.second
  27.6 0.0 collective-permute-done.2.far_second
  27.7 3.0 %near_second.1.near_field = f32[32,8,256]{2,1,0:T(8,128)S(1)} custom-call(s32[4,32]{1,0:T(4,128)} %bitcast.8, s32[2]{0:T(128)S(1)} %pad_add_fusion.place, bf16[32,8,256]{2,1,0:T(8,128)(2,1)S(1)} %copy-done.2, bf16[32,8,256]{2,1,0:T(8,128)(2,1)S(1)} %collective-permute-done.first, bf16[32,8,256]{2,1,0:T(8,128)(2,1)S(1)} %collective-permute-done.1.second, ...), custom_call_target="tpu_custom_call" | custom-call | flops 4600000000 | bytes 1000 | tf_op jit(solution)/shard_map/near_second/pallas_call | solution.py:196
  30.7 4.0 %all-to-all-done.recv = bf16[128,3,8,128]{3,2,1,0:T(8,128)(2,1)S(1)} async-done(((bf16[128,3,8,128]{3,2,1,0:T(8,128)(2,1)}), bf16[128,3,8,128]{3,2,1,0:T(8,128)(2,1)S(1)}, u32[]{:S(2)}, u32[]{:S(2)}) %all-to-all-start) | async-done | bytes 786464 | tf_op jit(solution)/shard_map/all_to_all | solution.py:278
  34.6 0.0 copy-done.1
  34.6 0.0 copy-done.3
  34.6 0.0 copy-done.4
  34.6 0.0 copy-done.5
  34.7 2.3 %final.1 = f32[32,8,256]{2,1,0:T(8,128)} custom-call(s32[1,6]{1,0:T(1,128)S(1)} %copy-done.5, bf16[128,3,8,128]{3,2,1,0:T(8,128)(2,1)S(1)} %all-to-all-done.recv, f32[32,8,256]{2,1,0:T(8,128)S(1)} %near_second.1.near_field, bf16[32,64,256]{2,1,0:T(8,128)(2,1)S(1)} %copy-done.1, bf16[1,6,64,64]{3,2,1,0:T(8,128)(2,1)S(1)} %copy-done.4, ...), custom_call_target="tpu_custom_call" | custom-call | tf_op jit(solution)/shard_map/final/pallas_call | solution.py:242
  (4 shorter events, 0.0 us)
Async XLA Ops:
  0.0 10.7 %copy-start.2 = (bf16[32,8,256]{2,1,0:T(8,128)(2,1)S(1)}, bf16[32,8,256]{2,1,0:T(8,128)(2,1)}, u32[]{:S(2)}) copy-start(bf16[32,8,256]{2,1,0:T(8,128)(2,1)} %charges.2) | copy-start | bytes 393220
  0.0 10.7 %copy-start.9 = (s32[32,8]{0,1:T(8,128)S(1)}, s32[32,8]{0,1:T(8,128)}, u32[]{:S(2)}) copy-start(s32[32,8]{0,1:T(8,128)} %param.17) | copy-start | bytes 3076
  0.0 10.7 %copy-start.10 = (s32[32,8]{0,1:T(8,128)S(1)}, s32[32,8]{0,1:T(8,128)}, u32[]{:S(2)}) copy-start(s32[32,8]{0,1:T(8,128)} %param.18) | copy-start | bytes 3076
  0.0 10.7 %copy-start.7 = (bf16[32,64,256]{2,1,0:T(8,128)(2,1)S(1)}, bf16[32,64,256]{2,1,0:T(8,128)(2,1)}, u32[]{:S(2)}) copy-start(bf16[32,64,256]{2,1,0:T(8,128)(2,1)} %basis.1) | copy-start | bytes 3145732
  0.0 10.7 %copy-start.6 = (bf16[32,8,64,64]{3,2,1,0:T(8,128)(2,1)S(1)}, bf16[32,8,64,64]{3,2,1,0:T(8,128)(2,1)}, u32[]{:S(2)}) copy-start(bf16[32,8,64,64]{3,2,1,0:T(8,128)(2,1)} %couplings.2) | copy-start | bytes 6291460
  0.0 10.7 %copy-start.8 = (bf16[32,64,64]{2,1,0:T(8,128)(2,1)S(1)}, bf16[32,64,64]{2,1,0:T(8,128)(2,1)}, u32[]{:S(2)}) copy-start(bf16[32,64,64]{2,1,0:T(8,128)(2,1)} %transfer.2) | copy-start | bytes 786436
  0.0 18.7 %collective-permute-start = (bf16[32,8,256]{2,1,0:T(8,128)(2,1)}, bf16[32,8,256]{2,1,0:T(8,128)(2,1)S(1)}, u32[]{:S(2)}, u32[]{:S(2)}) collective-permute-start(bf16[32,8,256]{2,1,0:T(8,128)(2,1)} %charges.2), channel_id=1, source_target_pairs={{0,1},{2,3},{4,5},{6,7},{8,9},{10,11},{12,13},{14,15},{16,17},{18,... | collective-permute-start | bytes 393224 | tf_op jit(solution)/shard_map/ppermute | solution.py:273
  2.2 25.4 %collective-permute-start.2 = (bf16[32,8,256]{2,1,0:T(8,128)(2,1)}, bf16[32,8,256]{2,1,0:T(8,128)(2,1)S(1)}, u32[]{:S(2)}, u32[]{:S(2)}) collective-permute-start(bf16[32,8,256]{2,1,0:T(8,128)(2,1)} %charges.2), channel_id=1, source_target_pairs={{15,16},{31,32},{47,48},{63,64},{79,80},{95,96},{111,112},{16,15},... | collective-permute-start | bytes 393224 | tf_op jit(solution)/shard_map/ppermute | solution.py:273
  14.0 20.7 %all-to-all-start = ((bf16[128,3,8,128]{3,2,1,0:T(8,128)(2,1)}), bf16[128,3,8,128]{3,2,1,0:T(8,128)(2,1)S(1)}, u32[]{:S(2)}, u32[]{:S(2)}) async-start(bf16[128,3,8,128]{3,2,1,0:T(8,128)(2,1)} %outgoing.1), calls=%async_computation | async-start | bytes 1572864 | tf_op jit(solution)/shard_map/all_to_all | solution.py:278
  18.0 9.7 %collective-permute-start.1 = (bf16[32,8,256]{2,1,0:T(8,128)(2,1)S(1)}, bf16[32,8,256]{2,1,0:T(8,128)(2,1)S(1)}, u32[]{:S(2)}, u32[]{:S(2)}) collective-permute-start(bf16[32,8,256]{2,1,0:T(8,128)(2,1)S(1)} %copy-done.2), channel_id=1, source_target_pairs={{1,2},{3,4},{5,6},{7,8},{9,10},{11,12},{13,14},{17,18},{19,20},{21... | collective-permute-start | bytes 393224 | tf_op jit(solution)/shard_map/ppermute | solution.py:279
  18.8 5.8 %copy-start = (bf16[32,4,256,256]{3,2,1,0:T(8,128)(2,1)S(1)}, bf16[32,4,256,256]{3,2,1,0:T(8,128)(2,1)}, u32[]{:S(2)}) copy-start(bf16[32,4,256,256]{3,2,1,0:T(8,128)(2,1)} %blocks.3) | copy-start | bytes 50331652
  24.5 10.1 %copy-start.1 = (bf16[32,64,256]{2,1,0:T(8,128)(2,1)S(1)}, bf16[32,64,256]{2,1,0:T(8,128)(2,1)}, u32[]{:S(2)}) copy-start(bf16[32,64,256]{2,1,0:T(8,128)(2,1)} %target_basis.1) | copy-start | bytes 3145732
  24.5 10.1 %copy-start.3 = (bf16[32,64,64]{2,1,0:T(8,128)(2,1)S(1)}, bf16[32,64,64]{2,1,0:T(8,128)(2,1)}, u32[]{:S(2)}) copy-start(bf16[32,64,64]{2,1,0:T(8,128)(2,1)} %transfer.3) | copy-start | bytes 786436
  24.5 10.1 %copy-start.4 = (bf16[1,6,64,64]{3,2,1,0:T(8,128)(2,1)S(1)}, bf16[1,6,64,64]{3,2,1,0:T(8,128)(2,1)}, u32[]{:S(2)}) copy-start(bf16[1,6,64,64]{3,2,1,0:T(8,128)(2,1)} %couplings.3) | copy-start | bytes 147460
  24.5 10.1 %copy-start.5 = (s32[1,6]{1,0:T(1,128)S(1)}, s32[1,6]{1,0:T(1,128)}, u32[]{:S(2)}) copy-start(s32[1,6]{1,0:T(1,128)} %coarse_list.1) | copy-start | bytes 76

commit v5 on v4

--- a/solution.py
+++ b/solution.py
@@ -157,52 +157,78 @@
     )(earlier, far_devices.T, far_slots.T, charges, source_basis, far_couplings, up_transfer)
 
 
-def near_terms(near_list, base, sources, blocks, l, js):
-    picked = [sources[near_list[j, l] - base] for j in js]
+def position():
+    return lax.axis_index(AXES)
+
+
+def near_term(source, blocks, l, j):
     half = POINTS // 2
-    return [
-        dot(picked[0], blocks[l, js[0], at : at + half], NT)
-        + dot(picked[1], blocks[l, js[1], at : at + half], NT)
-        for at in (0, half)
-    ]
-
-
-def near_first_kernel(near_list, place, charges, first, blocks, out, sources):
-    base, parity = place[0], place[1]
+    return [dot(source, blocks[l, j, at : at + half], NT) for at in (0, half)]
+
+
+def near_first_kernel(charges, first, blocks, out):
+    j = 2 - position() % 2
+    half = POINTS // 2
+    for l in range(LEAVES):
+        own = near_term(charges[l], blocks, l, 0)
+        other = near_term(first[l], blocks, l, j)
+        out[l, :, :half] = own[0] + other[0]
+        out[l, :, half:] = own[1] + other[1]
+
+
+def near_second_kernel(
+    near_list, charges, first, second, far_second, blocks, partial, out, sources, listed, sem
+):
+    copy = pltpu.make_async_copy(near_list, listed, sem)
+    copy.start()
+    me = position()
+    parity = me % 2
+    half = POINTS // 2
+    edge = jnp.where(me == 0, charges[0], jnp.where(me == DEVICES - 1, charges[LEAVES - 1], 0.0))
     sources[LEAVES : 2 * LEAVES] = charges[...]
     sources[pl.ds((1 - parity) * 2 * LEAVES, LEAVES)] = first[...]
     for l in range(LEAVES):
-        left, right = near_terms(near_list, base, sources, blocks, l, (0, 2 - parity))
-        out[l, :, : POINTS // 2] = left
-        out[l, :, POINTS // 2 :] = right
-
-
-def near_second_kernel(
-    near_list, place, charges, first, second, far_second, blocks, partial, out, sources
-):
-    base, parity = place[0], place[1]
-    sources[LEAVES : 2 * LEAVES] = charges[...]
-    sources[pl.ds((1 - parity) * 2 * LEAVES, LEAVES)] = first[...]
-    sources[pl.ds(parity * 2 * LEAVES, LEAVES)] = second[...] + far_second[...]
-    for l in range(LEAVES):
-        left, right = near_terms(near_list, base, sources, blocks, l, (1 + parity, NNEAR - 1))
-        out[l, :, : POINTS // 2] = partial[l, :, : POINTS // 2] + left
-        out[l, :, POINTS // 2 :] = partial[l, :, POINTS // 2 :] + right
-
-
-def near(kernel, name, near_list, place, *arrays):
-    vmem = pl.BlockSpec(memory_space=pltpu.VMEM)
-    smem = pl.BlockSpec(memory_space=pltpu.SMEM)
+        source = second[l] + far_second[l]
+        sources[parity * 2 * LEAVES + l] = source
+        term = near_term(source + edge, blocks, l, 1 + parity)
+        out[l, :, :half] = partial[l, :, :half] + term[0]
+        out[l, :, half:] = partial[l, :, half:] + term[1]
+    copy.wait()
+    base = me * LEAVES - LEAVES
+    for l in range(LEAVES):
+        term = near_term(sources[listed[NNEAR - 1, l] - base], blocks, l, NNEAR - 1)
+        out[l, :, :half] += term[0]
+        out[l, :, half:] += term[1]
+
+
+def near(kernel, name, arrays, scratch_shapes=()):
     return pl.pallas_call(
         kernel,
         out_shape=jax.ShapeDtypeStruct((LEAVES, RHS, POINTS), F32),
-        in_specs=[smem, smem] + [vmem] * len(arrays),
-        out_specs=vmem,
-        scratch_shapes=[pltpu.VMEM((3 * LEAVES, RHS, POINTS), BF16)],
+        in_specs=[pl.BlockSpec(memory_space=pltpu.VMEM)] * len(arrays),
+        out_specs=pl.BlockSpec(memory_space=pltpu.VMEM),
+        scratch_shapes=scratch_shapes,
         compiler_params=pltpu.CompilerParams(vmem_limit_bytes=20 * MIB),
         cost_estimate=pl.CostEstimate(flops=NEAR_FLOPS, bytes_accessed=1000, transcendentals=0),
         name=name,
-    )(*in_hbm(near_list.T), place, *arrays)
+    )(*arrays)
+
+
+def near_first(charges, first, near_blocks):
+    return near(near_first_kernel, "near_first", (charges, first, near_blocks))
+
+
+def near_second(near_list, charges, first, second, far_second, near_blocks, partial):
+    return near(
+        near_second_kernel,
+        "near_second",
+        (near_list.T, charges, first, second, far_second, near_blocks, partial),
+        (
+            pltpu.VMEM((3 * LEAVES, RHS, POINTS), BF16),
+            pltpu.SMEM((NNEAR, LEAVES), jnp.int32),
+            pltpu.SemaphoreType.DMA,
+        ),
+    )
 
 
 def unfold(rows):
@@ -210,10 +236,14 @@
 
 
 def final_kernel(coarse_list, recv, near_field, target_basis, couplings, transfer, out):
+    shape = (NCOARSE * 4, NCOARSE)
+    listed = jnp.where(iota(shape, 0) // 4 == iota(shape, 1), coarse_list[...], 0)
+    row_of = jnp.sum(listed, axis=1, keepdims=True) * 8 + iota((NCOARSE * 4, 1), 0) % 4
+    chosen = (iota((NCOARSE * 4, DEVICES * 8), 1) == row_of).astype(BF16)
+    picked = dot(chosen, recv[:, 2].reshape(DEVICES * 8, 128)).astype(BF16)
     coarse = jnp.zeros((RHS, RANK), F32)
     for j in range(NCOARSE):
-        picked = unfold(recv[coarse_list[0, j], 2].astype(F32)[:4]).astype(BF16)
-        coarse += dot(picked, couplings[0, j], NT)
+        coarse += dot(unfold(picked[4 * j : 4 * j + 4]), couplings[0, j], NT)
     lowered = dot(coarse.astype(BF16), transfer[...].reshape(LEAVES * RANK, RANK), NT)
 
     far = jnp.zeros((128, 128), F32)
@@ -238,11 +268,10 @@
 
 def final(coarse_list, recv, near_field, target_basis, coarse_couplings, down_transfer):
     vmem = pl.BlockSpec(memory_space=pltpu.VMEM)
-    smem = pl.BlockSpec(memory_space=pltpu.SMEM)
     return pl.pallas_call(
         final_kernel,
         out_shape=jax.ShapeDtypeStruct((LEAVES, RHS, POINTS), F32),
-        in_specs=[smem, vmem, vmem, vmem, vmem, vmem],
+        in_specs=[vmem] * 6,
         out_specs=vmem,
         compiler_params=pltpu.CompilerParams(vmem_limit_bytes=24 * MIB),
         name="final",
@@ -264,7 +293,6 @@
     down_transfer,
 ):
     count = lax.axis_size(AXES)
-    myself = lax.axis_index(AXES)
     of_subtree = lax.axis_size("dev")
     pairs = [[(i, i + 1) for i in range(start, count - 1, 2)] for start in (0, 1)]
     ends = [(i, j) for i, j in pairs[1] if j % of_subtree == 0]
@@ -277,20 +305,8 @@
     send, mine = lax.optimization_barrier((send, mine))
     recv = lax.all_to_all(send, AXES, 0, 0, tiled=True)
     second = lax.ppermute(mine, AXES, inner + [(j, i) for i, j in inner])
-    place = jnp.stack([myself * LEAVES - LEAVES, myself % 2])
-    partial = near(near_first_kernel, "near_first", near_list, place, mine, first, near_blocks)
-    near_field = near(
-        near_second_kernel,
-        "near_second",
-        near_list,
-        place,
-        mine,
-        first,
-        second,
-        far_second,
-        near_blocks,
-        partial,
-    )
+    partial = near_first(mine, first, near_blocks)
+    near_field = near_second(near_list, mine, first, second, far_second, near_blocks, partial)
     return final(coarse_list, recv, near_field, target_basis, coarse_couplings, down_transfer)
 
 

time: 37.2 us -> 36.8 us (0.989)
  Pallas kernels: 11.6 us -> 10.2 us
  waiting for transfers between devices: 4.01 us -> 5.12 us
    all_to_all x1, waiting for transfers between devices: 3.99 us -> 5.11 us  [body(): recv = lax.all_to_all(send, AXES, 0, 0, tiled=True)]
    pallas_call x2, Pallas kernels: 6.09 us -> 5.04 us  [near(): pl.pallas_call(kernel, out_shape=jax.ShapeDtypeStruct((LEAVES, RHS, POINT...]
    unnamed x22 -> x24, local copies, waits for them, and re-layouts: 5.81 us -> 5.83 us
  transfers between devices with their start and end apart: 4 -> 4, of which waited for: 1 -> 1; matrix products, arithmetic and copies ran while one was open for 0% -> 0% of each run, Pallas kernels for 25% -> 23%
where the time goes in v5:
time: 36.8 us; the launch traced here: 36.6 us
  starting transfers between devices  15.3 us (42%)
  Pallas kernels  10.2 us (28%)
  local copies, waits for them, and re-layouts  5.83 us (16%)
  waiting for transfers between devices  5.12 us (14%)
    ppermute x2, starting transfers between devices, body(): lax.ppermute(charges, AXES, some + [(j, i) for i, j in some])  10.6 us
    unnamed x24, local copies, waits for them, and re-layouts  5.83 us
    all_to_all x1, waiting for transfers between devices, body(): recv = lax.all_to_all(send, AXES, 0, 0, tiled=True)  5.11 us
    pallas_call x2, Pallas kernels, near(): pl.pallas_call(kernel, out_shape=jax.ShapeDtypeStruct((LEAVES, RHS, POINT...  5.04 us
    all_to_all x1, starting transfers between devices, body(): recv = lax.all_to_all(send, AXES, 0, 0, tiled=True)  4.01 us
    pallas_call x1, Pallas kernels, outgoing(): pl.pallas_call(outgoing_kernel, out_shape=jax.ShapeDtypeStruct((DEVICES,...  3.23 us
    pallas_call x1, Pallas kernels, final(): pl.pallas_call(final_kernel, out_shape=jax.ShapeDtypeStruct((LEAVES, RHS,...  1.96 us
  transfers between devices with their start and end apart: 4, of which 1 were waited for; matrix products, arithmetic and copies ran while one was open for 0% of the time, Pallas kernels for 23%

profile of v5, /device:TPU:1, one launch (start us, length us, event | category | flops | bytes accessed | tf_op | source)
XLA Modules:
  0.0 36.6 jit_solution(1540171561507112543)
XLA Ops:
  0.0 0.0 copy-start.2
  0.0 0.0 copy-start.8
  0.0 0.0 copy-start.7
  0.0 0.0 copy-start.9
  0.0 2.2 %collective-permute-start = (bf16[32,8,256]{2,1,0:T(8,128)(2,1)}, bf16[32,8,256]{2,1,0:T(8,128)(2,1)S(1)}, u32[]{:S(2)}, u32[]{:S(2)}) collective-permute-start(bf16[32,8,256]{2,1,0:T(8,128)(2,1)} %charges.2), channel_id=1, source_target_pairs={{0,1},{2,3},{4,5},{6,7},{8,9},{10,11},{12,13},{14,15},{16,17},{18,... | collective-permute-start | bytes 393224 | tf_op jit(solution)/shard_map/ppermute | solution.py:301
  2.2 8.4 %collective-permute-start.2 = (bf16[32,8,256]{2,1,0:T(8,128)(2,1)}, bf16[32,8,256]{2,1,0:T(8,128)(2,1)S(1)}, u32[]{:S(2)}, u32[]{:S(2)}) collective-permute-start(bf16[32,8,256]{2,1,0:T(8,128)(2,1)} %charges.2), channel_id=1, source_target_pairs={{15,16},{31,32},{47,48},{63,64},{79,80},{95,96},{111,112},{16,15},... | collective-permute-start | bytes 393224 | tf_op jit(solution)/shard_map/ppermute | solution.py:301
  10.7 0.0 copy-done.2
  10.7 0.0 copy-done.10
  10.7 0.0 copy-done.11
  10.7 0.0 copy-done.8
  10.7 0.0 copy-done.7
  10.7 0.0 copy-done.9
  10.7 0.0 copy-start.5
  10.7 3.2 %outgoing.1 = bf16[128,3,8,128]{3,2,1,0:T(8,128)(2,1)} custom-call(bf16[256,256]{1,0:T(8,128)(2,1)S(1)} %triangle.1.earlier, s32[8,32]{1,0:T(8,128)S(1)} %bitcast.4, s32[8,32]{1,0:T(8,128)S(1)} %bitcast.5, bf16[32,8,256]{2,1,0:T(8,128)(2,1)S(1)} %copy-done.2, bf16[32,64,256]{2,1,0:T(8,128)(2,1)S(1)} %copy-done.8, bf16[32,8,64,64]{3,2,1,0:T(8,128)(2,1)S(1)} %copy-done.7, ...), custom_call_target="tpu_custom_call" | custom-call | flops 26843545600 | bytes 1000 | tf_op jit(solution)/shard_map/outgoing/pallas_call | solution.py:144
  14.0 0.0 copy-start.1
  14.0 0.0 copy-start.3
  14.0 4.0 %all-to-all-start = ((bf16[128,3,8,128]{3,2,1,0:T(8,128)(2,1)}), bf16[128,3,8,128]{3,2,1,0:T(8,128)(2,1)S(1)}, u32[]{:S(2)}, u32[]{:S(2)}) async-start(bf16[128,3,8,128]{3,2,1,0:T(8,128)(2,1)} %outgoing.1), calls=%async_computation | async-start | bytes 1572864 | tf_op jit(solution)/shard_map/all_to_all | solution.py:306
  18.0 0.7 %collective-permute-start.1 = (bf16[32,8,256]{2,1,0:T(8,128)(2,1)S(1)}, bf16[32,8,256]{2,1,0:T(8,128)(2,1)S(1)}, u32[]{:S(2)}, u32[]{:S(2)}) collective-permute-start(bf16[32,8,256]{2,1,0:T(8,128)(2,1)S(1)} %copy-done.2), channel_id=1, source_target_pairs={{1,2},{3,4},{5,6},{7,8},{9,10},{11,12},{13,14},{17,18},{19,20},{21... | collective-permute-start | bytes 393224 | tf_op jit(solution)/shard_map/ppermute | solution.py:307
  18.7 0.0 collective-permute-done.first
  18.7 0.0 copy-start
  18.7 5.8 %copy-done = bf16[32,4,256,256]{3,2,1,0:T(8,128)(2,1)S(1)} copy-done((bf16[32,4,256,256]{3,2,1,0:T(8,128)(2,1)S(1)}, bf16[32,4,256,256]{3,2,1,0:T(8,128)(2,1)}, u32[]{:S(2)}) %copy-start) | copy-done | bytes 16777240
  24.5 2.3 %near_first.1.partial = f32[32,8,256]{2,1,0:T(8,128)S(1)} custom-call(bf16[32,8,256]{2,1,0:T(8,128)(2,1)S(1)} %copy-done.2, bf16[32,8,256]{2,1,0:T(8,128)(2,1)S(1)} %collective-permute-done.first, bf16[32,4,256,256]{3,2,1,0:T(8,128)(2,1)S(1)} %copy-done), custom_call_target="tpu_custom_call" | custom-call | flops 4600000000 | bytes 1000 | tf_op jit(solution)/shard_map/near_first/pallas_call | solution.py:205
  26.8 0.0 collective-permute-done.1.second
  26.8 0.0 collective-permute-done.2.far_second
  26.8 0.0 copy-done.5
  26.8 2.8 %near_second.1.near_field = f32[32,8,256]{2,1,0:T(8,128)S(1)} custom-call(s32[4,32]{1,0:T(4,128)S(1)} %bitcast.3, bf16[32,8,256]{2,1,0:T(8,128)(2,1)S(1)} %copy-done.2, bf16[32,8,256]{2,1,0:T(8,128)(2,1)S(1)} %collective-permute-done.first, bf16[32,8,256]{2,1,0:T(8,128)(2,1)S(1)} %collective-permute-done.1.second, ...), custom_call_target="tpu_custom_call" | custom-call | flops 4600000000 | bytes 1000 | tf_op jit(solution)/shard_map/near_second/pallas_call | solution.py:205
  29.5 5.1 %all-to-all-done.recv = bf16[128,3,8,128]{3,2,1,0:T(8,128)(2,1)S(1)} async-done(((bf16[128,3,8,128]{3,2,1,0:T(8,128)(2,1)}), bf16[128,3,8,128]{3,2,1,0:T(8,128)(2,1)S(1)}, u32[]{:S(2)}, u32[]{:S(2)}) %all-to-all-start) | async-done | bytes 786464 | tf_op jit(solution)/shard_map/all_to_all | solution.py:306
  34.7 0.0 copy-done.1
  34.7 0.0 copy-done.3
  34.7 0.0 copy-done.4
  34.7 0.0 copy-done.6
  34.7 2.0 %final.1 = f32[32,8,256]{2,1,0:T(8,128)} custom-call(s32[1,6]{1,0:T(1,128)S(1)} %copy-done.6, bf16[128,3,8,128]{3,2,1,0:T(8,128)(2,1)S(1)} %all-to-all-done.recv, f32[32,8,256]{2,1,0:T(8,128)S(1)} %near_second.1.near_field, bf16[32,64,256]{2,1,0:T(8,128)(2,1)S(1)} %copy-done.1, bf16[1,6,64,64]{3,2,1,0:T(8,128)(2,1)S(1)} %copy-done.4, ...), custom_call_target="tpu_custom_call" | custom-call | tf_op jit(solution)/shard_map/final/pallas_call | solution.py:271
  (5 shorter events, 0.0 us)
Async XLA Ops:
  0.0 10.7 %copy-start.2 = (bf16[32,8,256]{2,1,0:T(8,128)(2,1)S(1)}, bf16[32,8,256]{2,1,0:T(8,128)(2,1)}, u32[]{:S(2)}) copy-start(bf16[32,8,256]{2,1,0:T(8,128)(2,1)} %charges.2) | copy-start | bytes 393220
  0.0 10.7 %copy-start.10 = (s32[32,8]{0,1:T(8,128)S(1)}, s32[32,8]{0,1:T(8,128)}, u32[]{:S(2)}) copy-start(s32[32,8]{0,1:T(8,128)} %param.17) | copy-start | bytes 3076
  0.0 10.7 %copy-start.11 = (s32[32,8]{0,1:T(8,128)S(1)}, s32[32,8]{0,1:T(8,128)}, u32[]{:S(2)}) copy-start(s32[32,8]{0,1:T(8,128)} %param.18) | copy-start | bytes 3076
  0.0 10.7 %copy-start.8 = (bf16[32,64,256]{2,1,0:T(8,128)(2,1)S(1)}, bf16[32,64,256]{2,1,0:T(8,128)(2,1)}, u32[]{:S(2)}) copy-start(bf16[32,64,256]{2,1,0:T(8,128)(2,1)} %basis.1) | copy-start | bytes 3145732
  0.0 10.7 %copy-start.7 = (bf16[32,8,64,64]{3,2,1,0:T(8,128)(2,1)S(1)}, bf16[32,8,64,64]{3,2,1,0:T(8,128)(2,1)}, u32[]{:S(2)}) copy-start(bf16[32,8,64,64]{3,2,1,0:T(8,128)(2,1)} %couplings.2) | copy-start | bytes 6291460
  0.0 10.7 %copy-start.9 = (bf16[32,64,64]{2,1,0:T(8,128)(2,1)S(1)}, bf16[32,64,64]{2,1,0:T(8,128)(2,1)}, u32[]{:S(2)}) copy-start(bf16[32,64,64]{2,1,0:T(8,128)(2,1)} %transfer.2) | copy-start | bytes 786436
  0.0 18.6 %collective-permute-start = (bf16[32,8,256]{2,1,0:T(8,128)(2,1)}, bf16[32,8,256]{2,1,0:T(8,128)(2,1)S(1)}, u32[]{:S(2)}, u32[]{:S(2)}) collective-permute-start(bf16[32,8,256]{2,1,0:T(8,128)(2,1)} %charges.2), channel_id=1, source_target_pairs={{0,1},{2,3},{4,5},{6,7},{8,9},{10,11},{12,13},{14,15},{16,17},{18,... | collective-permute-start | bytes 393224 | tf_op jit(solution)/shard_map/ppermute | solution.py:301
  2.2 24.5 %collective-permute-start.2 = (bf16[32,8,256]{2,1,0:T(8,128)(2,1)}, bf16[32,8,256]{2,1,0:T(8,128)(2,1)S(1)}, u32[]{:S(2)}, u32[]{:S(2)}) collective-permute-start(bf16[32,8,256]{2,1,0:T(8,128)(2,1)} %charges.2), channel_id=1, source_target_pairs={{15,16},{31,32},{47,48},{63,64},{79,80},{95,96},{111,112},{16,15},... | collective-permute-start | bytes 393224 | tf_op jit(solution)/shard_map/ppermute | solution.py:301
  10.7 16.1 %copy-start.5 = (s32[32,4]{0,1:T(4,128)S(1)}, s32[32,4]{0,1:T(4,128)}, u32[]{:S(2)}) copy-start(s32[32,4]{0,1:T(4,128)} %param.13) | copy-start | bytes 1540
  14.0 20.7 %copy-start.1 = (bf16[32,64,256]{2,1,0:T(8,128)(2,1)S(1)}, bf16[32,64,256]{2,1,0:T(8,128)(2,1)}, u32[]{:S(2)}) copy-start(bf16[32,64,256]{2,1,0:T(8,128)(2,1)} %target_basis.1) | copy-start | bytes 3145732
  14.0 20.7 %copy-start.3 = (bf16[32,64,64]{2,1,0:T(8,128)(2,1)S(1)}, bf16[32,64,64]{2,1,0:T(8,128)(2,1)}, u32[]{:S(2)}) copy-start(bf16[32,64,64]{2,1,0:T(8,128)(2,1)} %transfer.3) | copy-start | bytes 786436
  14.0 20.7 %all-to-all-start = ((bf16[128,3,8,128]{3,2,1,0:T(8,128)(2,1)}), bf16[128,3,8,128]{3,2,1,0:T(8,128)(2,1)S(1)}, u32[]{:S(2)}, u32[]{:S(2)}) async-start(bf16[128,3,8,128]{3,2,1,0:T(8,128)(2,1)} %outgoing.1), calls=%async_computation | async-start | bytes 1572864 | tf_op jit(solution)/shard_map/all_to_all | solution.py:306
  18.0 8.8 %collective-permute-start.1 = (bf16[32,8,256]{2,1,0:T(8,128)(2,1)S(1)}, bf16[32,8,256]{2,1,0:T(8,128)(2,1)S(1)}, u32[]{:S(2)}, u32[]{:S(2)}) collective-permute-start(bf16[32,8,256]{2,1,0:T(8,128)(2,1)S(1)} %copy-done.2), channel_id=1, source_target_pairs={{1,2},{3,4},{5,6},{7,8},{9,10},{11,12},{13,14},{17,18},{19,20},{21... | collective-permute-start | bytes 393224 | tf_op jit(solution)/shard_map/ppermute | solution.py:307
  18.7 5.8 %copy-start = (bf16[32,4,256,256]{3,2,1,0:T(8,128)(2,1)S(1)}, bf16[32,4,256,256]{3,2,1,0:T(8,128)(2,1)}, u32[]{:S(2)}) copy-start(bf16[32,4,256,256]{3,2,1,0:T(8,128)(2,1)} %blocks.3) | copy-start | bytes 50331652
  24.5 10.2 %copy-start.4 = (bf16[1,6,64,64]{3,2,1,0:T(8,128)(2,1)S(1)}, bf16[1,6,64,64]{3,2,1,0:T(8,128)(2,1)}, u32[]{:S(2)}) copy-start(bf16[1,6,64,64]{3,2,1,0:T(8,128)(2,1)} %couplings.3) | copy-start | bytes 147460
  24.5 10.2 %copy-start.6 = (s32[1,6]{1,0:T(1,128)S(1)}, s32[1,6]{1,0:T(1,128)}, u32[]{:S(2)}) copy-start(s32[1,6]{1,0:T(1,128)} %coarse_list.1) | copy-start | bytes 76

commit v6 on v5

--- a/solution.py
+++ b/solution.py
@@ -239,31 +239,46 @@
     shape = (NCOARSE * 4, NCOARSE)
     listed = jnp.where(iota(shape, 0) // 4 == iota(shape, 1), coarse_list[...], 0)
     row_of = jnp.sum(listed, axis=1, keepdims=True) * 8 + iota((NCOARSE * 4, 1), 0) % 4
-    chosen = (iota((NCOARSE * 4, DEVICES * 8), 1) == row_of).astype(BF16)
-    picked = dot(chosen, recv[:, 2].reshape(DEVICES * 8, 128)).astype(BF16)
-    coarse = jnp.zeros((RHS, RANK), F32)
-    for j in range(NCOARSE):
-        coarse += dot(unfold(picked[4 * j : 4 * j + 4]), couplings[0, j], NT)
-    lowered = dot(coarse.astype(BF16), transfer[...].reshape(LEAVES * RANK, RANK), NT)
-
-    far = jnp.zeros((128, 128), F32)
+    node = (iota((NCOARSE * 4, DEVICES * 8), 1) == row_of).astype(BF16)
+
     span = 32
     lane = iota((span, 8, 128), 2)
     place = iota((span, 8, 128), 1)
-    for at in range(0, DEVICES, span):
+    piece = [lane % 4 == 2 * g + place // 4 for g in range(2)]
+    slot = (lane // 4 + 1).astype(F32)
+
+    def far_part(at):
         part = pl.ds(at, span)
         names = recv[part, 2].astype(F32)
-        names = jnp.where(place >= 4, names, pltpu.roll(names, 4, 1)).astype(jnp.int32) - 1
-        same = names == lane // 4
-        for g in range(2):
-            chosen = (same & (lane % 4 == 2 * g + place // 4)).astype(F32)
-            far += dot(
-                chosen.reshape(span * 8, 128).astype(BF16), recv[part, g].reshape(span * 8, 128), TN
+        same = jnp.where(place >= 4, names, pltpu.roll(names, 4, 1)) == slot
+        terms = [
+            dot(
+                jnp.where(same & piece[g], 1.0, 0.0).reshape(span * 8, 128).astype(BF16),
+                recv[part, g].reshape(span * 8, 128),
+                TN,
             )
-    for l in range(LEAVES):
-        rows = unfold(far[l * 4 : (l + 1) * 4, :])
-        local = (rows + lowered[:, l * RANK : (l + 1) * RANK]).astype(BF16)
-        out[l] = near_field[l] + dot(local, target_basis[l])
+            for g in range(2)
+        ]
+        return terms[0] + terms[1]
+
+    picked = dot(node, recv[:, 2].reshape(DEVICES * 8, 128)).astype(BF16)
+    far = far_part(0)
+    coarse = [dot(unfold(picked[4 * j : 4 * j + 4]), couplings[0, j], NT) for j in range(NCOARSE)]
+    far += far_part(span)
+    coarse = ((coarse[0] + coarse[1]) + (coarse[2] + coarse[3])) + (coarse[4] + coarse[5])
+    far += far_part(2 * span)
+    lowered = dot(coarse.astype(BF16), transfer[...].reshape(LEAVES * RANK, RANK), NT)
+    far += far_part(3 * span)
+    upper = iota((RHS, 128), 0) < 4
+    for l in range(0, LEAVES, 2):
+        rows = far[l * 4 : l * 4 + 8, :]
+        swapped = pltpu.roll(rows, RANK, 1)
+        turned = pltpu.roll(rows, 4, 0)
+        pair = lowered[:, l * RANK : (l + 2) * RANK]
+        even = jnp.where(upper, rows, pltpu.roll(swapped, 4, 0)) + pair
+        odd = jnp.where(upper, turned, swapped) + pltpu.roll(pair, RANK, 1)
+        for i, local in enumerate((even, odd)):
+            out[l + i] = near_field[l + i] + dot(local[:, :RANK].astype(BF16), target_basis[l + i])
 
 
 def final(coarse_list, recv, near_field, target_basis, coarse_couplings, down_transfer):

time: 36.8 us -> 36.7 us (level)
  no operation moved by 1% of the time
where the time goes in v6:
time: 36.7 us; the launch traced here: 36.5 us
  starting transfers between devices  15.3 us (42%)
  Pallas kernels  10.1 us (28%)
  local copies, waits for them, and re-layouts  5.83 us (16%)
  waiting for transfers between devices  5.12 us (14%)
    ppermute x2, starting transfers between devices, body(): lax.ppermute(charges, AXES, some + [(j, i) for i, j in some])  10.6 us
    unnamed x24, local copies, waits for them, and re-layouts  5.83 us
    all_to_all x1, waiting for transfers between devices, body(): recv = lax.all_to_all(send, AXES, 0, 0, tiled=True)  5.11 us
    pallas_call x2, Pallas kernels, near(): pl.pallas_call(kernel, out_shape=jax.ShapeDtypeStruct((LEAVES, RHS, POINT...  5.04 us
    all_to_all x1, starting transfers between devices, body(): recv = lax.all_to_all(send, AXES, 0, 0, tiled=True)  4.01 us
    pallas_call x1, Pallas kernels, outgoing(): pl.pallas_call(outgoing_kernel, out_shape=jax.ShapeDtypeStruct((DEVICES,...  3.23 us
    pallas_call x1, Pallas kernels, final(): pl.pallas_call(final_kernel, out_shape=jax.ShapeDtypeStruct((LEAVES, RHS,...  1.79 us
  transfers between devices with their start and end apart: 4, of which 1 were waited for; matrix products, arithmetic and copies ran while one was open for 0% of the time, Pallas kernels for 23%

profile of v6, /device:TPU:1, one launch (start us, length us, event | category | flops | bytes accessed | tf_op | source)
XLA Modules:
  0.0 36.5 jit_solution(1016866631481078580)
XLA Ops:
  0.0 0.0 copy-start.2
  0.0 0.0 copy-start.8
  0.0 0.0 copy-start.7
  0.0 0.0 copy-start.9
  0.0 2.2 %collective-permute-start = (bf16[32,8,256]{2,1,0:T(8,128)(2,1)}, bf16[32,8,256]{2,1,0:T(8,128)(2,1)S(1)}, u32[]{:S(2)}, u32[]{:S(2)}) collective-permute-start(bf16[32,8,256]{2,1,0:T(8,128)(2,1)} %charges.2), channel_id=1, source_target_pairs={{0,1},{2,3},{4,5},{6,7},{8,9},{10,11},{12,13},{14,15},{16,17},{18,... | collective-permute-start | bytes 393224 | tf_op jit(solution)/shard_map/ppermute | solution.py:316
  2.2 8.4 %collective-permute-start.2 = (bf16[32,8,256]{2,1,0:T(8,128)(2,1)}, bf16[32,8,256]{2,1,0:T(8,128)(2,1)S(1)}, u32[]{:S(2)}, u32[]{:S(2)}) collective-permute-start(bf16[32,8,256]{2,1,0:T(8,128)(2,1)} %charges.2), channel_id=1, source_target_pairs={{15,16},{31,32},{47,48},{63,64},{79,80},{95,96},{111,112},{16,15},... | collective-permute-start | bytes 393224 | tf_op jit(solution)/shard_map/ppermute | solution.py:316
  10.7 0.0 copy-done.2
  10.7 0.0 copy-done.10
  10.7 0.0 copy-done.11
  10.7 0.0 copy-done.8
  10.7 0.0 copy-done.7
  10.7 0.0 copy-done.9
  10.7 0.0 copy-start.5
  10.7 3.2 %outgoing.1 = bf16[128,3,8,128]{3,2,1,0:T(8,128)(2,1)} custom-call(bf16[256,256]{1,0:T(8,128)(2,1)S(1)} %triangle.1.earlier, s32[8,32]{1,0:T(8,128)S(1)} %bitcast.4, s32[8,32]{1,0:T(8,128)S(1)} %bitcast.5, bf16[32,8,256]{2,1,0:T(8,128)(2,1)S(1)} %copy-done.2, bf16[32,64,256]{2,1,0:T(8,128)(2,1)S(1)} %copy-done.8, bf16[32,8,64,64]{3,2,1,0:T(8,128)(2,1)S(1)} %copy-done.7, ...), custom_call_target="tpu_custom_call" | custom-call | flops 26843545600 | bytes 1000 | tf_op jit(solution)/shard_map/outgoing/pallas_call | solution.py:144
  14.0 0.0 copy-start.1
  14.0 0.0 copy-start.3
  14.0 4.0 %all-to-all-start = ((bf16[128,3,8,128]{3,2,1,0:T(8,128)(2,1)}), bf16[128,3,8,128]{3,2,1,0:T(8,128)(2,1)S(1)}, u32[]{:S(2)}, u32[]{:S(2)}) async-start(bf16[128,3,8,128]{3,2,1,0:T(8,128)(2,1)} %outgoing.1), calls=%async_computation | async-start | bytes 1572864 | tf_op jit(solution)/shard_map/all_to_all | solution.py:321
  18.0 0.7 %collective-permute-start.1 = (bf16[32,8,256]{2,1,0:T(8,128)(2,1)S(1)}, bf16[32,8,256]{2,1,0:T(8,128)(2,1)S(1)}, u32[]{:S(2)}, u32[]{:S(2)}) collective-permute-start(bf16[32,8,256]{2,1,0:T(8,128)(2,1)S(1)} %copy-done.2), channel_id=1, source_target_pairs={{1,2},{3,4},{5,6},{7,8},{9,10},{11,12},{13,14},{17,18},{19,20},{21... | collective-permute-start | bytes 393224 | tf_op jit(solution)/shard_map/ppermute | solution.py:322
  18.7 0.0 collective-permute-done.first
  18.7 0.0 copy-start
  18.7 5.8 %copy-done = bf16[32,4,256,256]{3,2,1,0:T(8,128)(2,1)S(1)} copy-done((bf16[32,4,256,256]{3,2,1,0:T(8,128)(2,1)S(1)}, bf16[32,4,256,256]{3,2,1,0:T(8,128)(2,1)}, u32[]{:S(2)}) %copy-start) | copy-done | bytes 16777240
  24.5 2.3 %near_first.1.partial = f32[32,8,256]{2,1,0:T(8,128)S(1)} custom-call(bf16[32,8,256]{2,1,0:T(8,128)(2,1)S(1)} %copy-done.2, bf16[32,8,256]{2,1,0:T(8,128)(2,1)S(1)} %collective-permute-done.first, bf16[32,4,256,256]{3,2,1,0:T(8,128)(2,1)S(1)} %copy-done), custom_call_target="tpu_custom_call" | custom-call | flops 4600000000 | bytes 1000 | tf_op jit(solution)/shard_map/near_first/pallas_call | solution.py:205
  26.8 0.0 collective-permute-done.1.second
  26.8 0.0 collective-permute-done.2.far_second
  26.8 0.0 copy-done.5
  26.8 2.8 %near_second.1.near_field = f32[32,8,256]{2,1,0:T(8,128)S(1)} custom-call(s32[4,32]{1,0:T(4,128)S(1)} %bitcast.3, bf16[32,8,256]{2,1,0:T(8,128)(2,1)S(1)} %copy-done.2, bf16[32,8,256]{2,1,0:T(8,128)(2,1)S(1)} %collective-permute-done.first, bf16[32,8,256]{2,1,0:T(8,128)(2,1)S(1)} %collective-permute-done.1.second, ...), custom_call_target="tpu_custom_call" | custom-call | flops 4600000000 | bytes 1000 | tf_op jit(solution)/shard_map/near_second/pallas_call | solution.py:205
  29.5 5.1 %all-to-all-done.recv = bf16[128,3,8,128]{3,2,1,0:T(8,128)(2,1)S(1)} async-done(((bf16[128,3,8,128]{3,2,1,0:T(8,128)(2,1)}), bf16[128,3,8,128]{3,2,1,0:T(8,128)(2,1)S(1)}, u32[]{:S(2)}, u32[]{:S(2)}) %all-to-all-start) | async-done | bytes 786464 | tf_op jit(solution)/shard_map/all_to_all | solution.py:321
  34.7 0.0 copy-done.1
  34.7 0.0 copy-done.3
  34.7 0.0 copy-done.4
  34.7 0.0 copy-done.6
  34.7 1.8 %final.1 = f32[32,8,256]{2,1,0:T(8,128)} custom-call(s32[1,6]{1,0:T(1,128)S(1)} %copy-done.6, bf16[128,3,8,128]{3,2,1,0:T(8,128)(2,1)S(1)} %all-to-all-done.recv, f32[32,8,256]{2,1,0:T(8,128)S(1)} %near_second.1.near_field, bf16[32,64,256]{2,1,0:T(8,128)(2,1)S(1)} %copy-done.1, bf16[1,6,64,64]{3,2,1,0:T(8,128)(2,1)S(1)} %copy-done.4, ...), custom_call_target="tpu_custom_call" | custom-call | tf_op jit(solution)/shard_map/final/pallas_call | solution.py:286
  (5 shorter events, 0.0 us)
Async XLA Ops:
  0.0 10.7 %copy-start.2 = (bf16[32,8,256]{2,1,0:T(8,128)(2,1)S(1)}, bf16[32,8,256]{2,1,0:T(8,128)(2,1)}, u32[]{:S(2)}) copy-start(bf16[32,8,256]{2,1,0:T(8,128)(2,1)} %charges.2) | copy-start | bytes 393220
  0.0 10.7 %copy-start.10 = (s32[32,8]{0,1:T(8,128)S(1)}, s32[32,8]{0,1:T(8,128)}, u32[]{:S(2)}) copy-start(s32[32,8]{0,1:T(8,128)} %param.17) | copy-start | bytes 3076
  0.0 10.7 %copy-start.11 = (s32[32,8]{0,1:T(8,128)S(1)}, s32[32,8]{0,1:T(8,128)}, u32[]{:S(2)}) copy-start(s32[32,8]{0,1:T(8,128)} %param.18) | copy-start | bytes 3076
  0.0 10.7 %copy-start.8 = (bf16[32,64,256]{2,1,0:T(8,128)(2,1)S(1)}, bf16[32,64,256]{2,1,0:T(8,128)(2,1)}, u32[]{:S(2)}) copy-start(bf16[32,64,256]{2,1,0:T(8,128)(2,1)} %basis.1) | copy-start | bytes 3145732
  0.0 10.7 %copy-start.7 = (bf16[32,8,64,64]{3,2,1,0:T(8,128)(2,1)S(1)}, bf16[32,8,64,64]{3,2,1,0:T(8,128)(2,1)}, u32[]{:S(2)}) copy-start(bf16[32,8,64,64]{3,2,1,0:T(8,128)(2,1)} %couplings.2) | copy-start | bytes 6291460
  0.0 10.7 %copy-start.9 = (bf16[32,64,64]{2,1,0:T(8,128)(2,1)S(1)}, bf16[32,64,64]{2,1,0:T(8,128)(2,1)}, u32[]{:S(2)}) copy-start(bf16[32,64,64]{2,1,0:T(8,128)(2,1)} %transfer.2) | copy-start | bytes 786436
  0.0 18.6 %collective-permute-start = (bf16[32,8,256]{2,1,0:T(8,128)(2,1)}, bf16[32,8,256]{2,1,0:T(8,128)(2,1)S(1)}, u32[]{:S(2)}, u32[]{:S(2)}) collective-permute-start(bf16[32,8,256]{2,1,0:T(8,128)(2,1)} %charges.2), channel_id=1, source_target_pairs={{0,1},{2,3},{4,5},{6,7},{8,9},{10,11},{12,13},{14,15},{16,17},{18,... | collective-permute-start | bytes 393224 | tf_op jit(solution)/shard_map/ppermute | solution.py:316
  2.2 24.5 %collective-permute-start.2 = (bf16[32,8,256]{2,1,0:T(8,128)(2,1)}, bf16[32,8,256]{2,1,0:T(8,128)(2,1)S(1)}, u32[]{:S(2)}, u32[]{:S(2)}) collective-permute-start(bf16[32,8,256]{2,1,0:T(8,128)(2,1)} %charges.2), channel_id=1, source_target_pairs={{15,16},{31,32},{47,48},{63,64},{79,80},{95,96},{111,112},{16,15},... | collective-permute-start | bytes 393224 | tf_op jit(solution)/shard_map/ppermute | solution.py:316
  10.7 16.1 %copy-start.5 = (s32[32,4]{0,1:T(4,128)S(1)}, s32[32,4]{0,1:T(4,128)}, u32[]{:S(2)}) copy-start(s32[32,4]{0,1:T(4,128)} %param.13) | copy-start | bytes 1540
  14.0 20.7 %copy-start.1 = (bf16[32,64,256]{2,1,0:T(8,128)(2,1)S(1)}, bf16[32,64,256]{2,1,0:T(8,128)(2,1)}, u32[]{:S(2)}) copy-start(bf16[32,64,256]{2,1,0:T(8,128)(2,1)} %target_basis.1) | copy-start | bytes 3145732
  14.0 20.7 %copy-start.3 = (bf16[32,64,64]{2,1,0:T(8,128)(2,1)S(1)}, bf16[32,64,64]{2,1,0:T(8,128)(2,1)}, u32[]{:S(2)}) copy-start(bf16[32,64,64]{2,1,0:T(8,128)(2,1)} %transfer.3) | copy-start | bytes 786436
  14.0 20.7 %all-to-all-start = ((bf16[128,3,8,128]{3,2,1,0:T(8,128)(2,1)}), bf16[128,3,8,128]{3,2,1,0:T(8,128)(2,1)S(1)}, u32[]{:S(2)}, u32[]{:S(2)}) async-start(bf16[128,3,8,128]{3,2,1,0:T(8,128)(2,1)} %outgoing.1), calls=%async_computation | async-start | bytes 1572864 | tf_op jit(solution)/shard_map/all_to_all | solution.py:321
  18.0 8.8 %collective-permute-start.1 = (bf16[32,8,256]{2,1,0:T(8,128)(2,1)S(1)}, bf16[32,8,256]{2,1,0:T(8,128)(2,1)S(1)}, u32[]{:S(2)}, u32[]{:S(2)}) collective-permute-start(bf16[32,8,256]{2,1,0:T(8,128)(2,1)S(1)} %copy-done.2), channel_id=1, source_target_pairs={{1,2},{3,4},{5,6},{7,8},{9,10},{11,12},{13,14},{17,18},{19,20},{21... | collective-permute-start | bytes 393224 | tf_op jit(solution)/shard_map/ppermute | solution.py:322
  18.7 5.8 %copy-start = (bf16[32,4,256,256]{3,2,1,0:T(8,128)(2,1)S(1)}, bf16[32,4,256,256]{3,2,1,0:T(8,128)(2,1)}, u32[]{:S(2)}) copy-start(bf16[32,4,256,256]{3,2,1,0:T(8,128)(2,1)} %blocks.3) | copy-start | bytes 50331652
  24.5 10.2 %copy-start.4 = (bf16[1,6,64,64]{3,2,1,0:T(8,128)(2,1)S(1)}, bf16[1,6,64,64]{3,2,1,0:T(8,128)(2,1)}, u32[]{:S(2)}) copy-start(bf16[1,6,64,64]{3,2,1,0:T(8,128)(2,1)} %couplings.3) | copy-start | bytes 147460
  24.5 10.2 %copy-start.6 = (s32[1,6]{1,0:T(1,128)S(1)}, s32[1,6]{1,0:T(1,128)}, u32[]{:S(2)}) copy-start(s32[1,6]{1,0:T(1,128)} %coarse_list.1) | copy-start | bytes 76

commit v7 on v6

--- a/solution.py
+++ b/solution.py
@@ -97,12 +97,16 @@
     writes = [pltpu.make_async_copy(send.at[:, 2], send_hbm.at[:, 2], sems.at[0])]
     writes[0].start()
 
-    for l in range(LEAVES):
+    shape = (2 * RHS, 128)
+    own_half = (iota(shape, 0) < RHS) == (iota(shape, 1) < RANK)
+    for l in range(0, LEAVES, 2):
+        both = jnp.concatenate(moments[l : l + 2], axis=0).astype(F32)
+        both = jnp.where(own_half, jnp.concatenate([both, both], axis=1), 0.0).astype(BF16)
         for h in range(2):
-            half = couplings[l, h * 4 : h * 4 + 4].reshape(4 * RANK, RANK)
-            product = dot(moments[l], half, NT)
+            pair = [couplings[l + i, h * 4 : h * 4 + 4].reshape(4 * RANK, RANK) for i in range(2)]
+            product = dot(both, jnp.concatenate(pair, axis=1), NT)
             for t in range(2):
-                products[2 * h + t, l * RHS : (l + 1) * RHS, :] = product[:, t * 128 : (t + 1) * 128]
+                products[2 * h + t, l * RHS : (l + 2) * RHS, :] = product[:, t * 128 : (t + 1) * 128]
 
     low = iota((LEAVES, 128), 1) < RANK
     pieces = []
@@ -262,13 +266,10 @@
         return terms[0] + terms[1]
 
     picked = dot(node, recv[:, 2].reshape(DEVICES * 8, 128)).astype(BF16)
-    far = far_part(0)
+    far = (far_part(0) + far_part(span)) + (far_part(2 * span) + far_part(3 * span))
     coarse = [dot(unfold(picked[4 * j : 4 * j + 4]), couplings[0, j], NT) for j in range(NCOARSE)]
-    far += far_part(span)
     coarse = ((coarse[0] + coarse[1]) + (coarse[2] + coarse[3])) + (coarse[4] + coarse[5])
-    far += far_part(2 * span)
     lowered = dot(coarse.astype(BF16), transfer[...].reshape(LEAVES * RANK, RANK), NT)
-    far += far_part(3 * span)
     upper = iota((RHS, 128), 0) < 4
     for l in range(0, LEAVES, 2):
         rows = far[l * 4 : l * 4 + 8, :]

time: 36.7 us -> 36.1 us (0.984)
  Pallas kernels: 10.1 us -> 9.46 us
    pallas_call x1, Pallas kernels: 3.23 us -> 2.7 us  [outgoing(): pl.pallas_call(outgoing_kernel, out_shape=jax.ShapeDtypeStruct((DEVICES,...]
  transfers between devices with their start and end apart: 4 -> 4, of which waited for: 1 -> 1; matrix products, arithmetic and copies ran while one was open for 0% -> 0% of each run, Pallas kernels for 23% -> 22%
where the time goes in v7:
time: 36.1 us; the launch traced here: 35.9 us
  starting transfers between devices  15.3 us (42%)
  Pallas kernels  9.46 us (26%)
  local copies, waits for them, and re-layouts  5.83 us (16%)
  waiting for transfers between devices  5.12 us (14%)
    ppermute x2, starting transfers between devices, body(): lax.ppermute(charges, AXES, some + [(j, i) for i, j in some])  10.6 us
    unnamed x24, local copies, waits for them, and re-layouts  5.83 us
    all_to_all x1, waiting for transfers between devices, body(): recv = lax.all_to_all(send, AXES, 0, 0, tiled=True)  5.12 us
    pallas_call x2, Pallas kernels, near(): pl.pallas_call(kernel, out_shape=jax.ShapeDtypeStruct((LEAVES, RHS, POINT...  5.04 us
    all_to_all x1, starting transfers between devices, body(): recv = lax.all_to_all(send, AXES, 0, 0, tiled=True)  4.01 us
    pallas_call x1, Pallas kernels, outgoing(): pl.pallas_call(outgoing_kernel, out_shape=jax.ShapeDtypeStruct((DEVICES,...  2.7 us
    pallas_call x1, Pallas kernels, final(): pl.pallas_call(final_kernel, out_shape=jax.ShapeDtypeStruct((LEAVES, RHS,...  1.7 us
  transfers between devices with their start and end apart: 4, of which 1 were waited for; matrix products, arithmetic and copies ran while one was open for 0% of the time, Pallas kernels for 22%

profile of v7, /device:TPU:1, one launch (start us, length us, event | category | flops | bytes accessed | tf_op | source)
XLA Modules:
  0.0 35.9 jit_solution(7450241850551750822)
XLA Ops:
  0.0 0.0 copy-start.10
  0.0 0.0 copy-start.8
  0.0 0.0 copy-start.7
  0.0 0.0 copy-start.9
  0.0 2.2 %collective-permute-start = (bf16[32,8,256]{2,1,0:T(8,128)(2,1)}, bf16[32,8,256]{2,1,0:T(8,128)(2,1)S(1)}, u32[]{:S(2)}, u32[]{:S(2)}) collective-permute-start(bf16[32,8,256]{2,1,0:T(8,128)(2,1)} %charges.2), channel_id=1, source_target_pairs={{0,1},{2,3},{4,5},{6,7},{8,9},{10,11},{12,13},{14,15},{16,17},{18,... | collective-permute-start | bytes 393224 | tf_op jit(solution)/shard_map/ppermute | solution.py:317
  2.2 8.4 %collective-permute-start.2 = (bf16[32,8,256]{2,1,0:T(8,128)(2,1)}, bf16[32,8,256]{2,1,0:T(8,128)(2,1)S(1)}, u32[]{:S(2)}, u32[]{:S(2)}) collective-permute-start(bf16[32,8,256]{2,1,0:T(8,128)(2,1)} %charges.2), channel_id=1, source_target_pairs={{15,16},{31,32},{47,48},{63,64},{79,80},{95,96},{111,112},{16,15},... | collective-permute-start | bytes 393224 | tf_op jit(solution)/shard_map/ppermute | solution.py:317
  10.7 0.0 copy-done.2
  10.7 0.0 copy-done.10
  10.7 0.0 copy-done.11
  10.7 0.0 copy-done.8
  10.7 0.0 copy-done.7
  10.7 0.0 copy-done.9
  10.7 0.0 copy-start.5
  10.7 2.7 %outgoing.1 = bf16[128,3,8,128]{3,2,1,0:T(8,128)(2,1)} custom-call(bf16[256,256]{1,0:T(8,128)(2,1)S(1)} %triangle.1.earlier, s32[8,32]{1,0:T(8,128)S(1)} %bitcast.4, s32[8,32]{1,0:T(8,128)S(1)} %bitcast.5, bf16[32,8,256]{2,1,0:T(8,128)(2,1)S(1)} %copy-done.2, bf16[32,64,256]{2,1,0:T(8,128)(2,1)S(1)} %copy-done.8, bf16[32,8,64,64]{3,2,1,0:T(8,128)(2,1)S(1)} %copy-done.7, ...), custom_call_target="tpu_custom_call" | custom-call | flops 26843545600 | bytes 1000 | tf_op jit(solution)/shard_map/outgoing/pallas_call | solution.py:148
  13.4 0.0 copy-start.1
  13.4 0.0 copy-start.3
  13.5 4.0 %all-to-all-start = ((bf16[128,3,8,128]{3,2,1,0:T(8,128)(2,1)}), bf16[128,3,8,128]{3,2,1,0:T(8,128)(2,1)S(1)}, u32[]{:S(2)}, u32[]{:S(2)}) async-start(bf16[128,3,8,128]{3,2,1,0:T(8,128)(2,1)} %outgoing.1), calls=%async_computation | async-start | bytes 1572864 | tf_op jit(solution)/shard_map/all_to_all | solution.py:322
  17.5 0.7 %collective-permute-start.1 = (bf16[32,8,256]{2,1,0:T(8,128)(2,1)S(1)}, bf16[32,8,256]{2,1,0:T(8,128)(2,1)S(1)}, u32[]{:S(2)}, u32[]{:S(2)}) collective-permute-start(bf16[32,8,256]{2,1,0:T(8,128)(2,1)S(1)} %copy-done.2), channel_id=1, source_target_pairs={{1,2},{3,4},{5,6},{7,8},{9,10},{11,12},{13,14},{17,18},{19,20},{21... | collective-permute-start | bytes 393224 | tf_op jit(solution)/shard_map/ppermute | solution.py:323
  18.2 0.0 collective-permute-done.first
  18.2 0.0 copy-start
  18.2 5.8 %copy-done = bf16[32,4,256,256]{3,2,1,0:T(8,128)(2,1)S(1)} copy-done((bf16[32,4,256,256]{3,2,1,0:T(8,128)(2,1)S(1)}, bf16[32,4,256,256]{3,2,1,0:T(8,128)(2,1)}, u32[]{:S(2)}) %copy-start) | copy-done | bytes 16777240
  23.9 2.3 %near_first.1.partial = f32[32,8,256]{2,1,0:T(8,128)S(1)} custom-call(bf16[32,8,256]{2,1,0:T(8,128)(2,1)S(1)} %copy-done.2, bf16[32,8,256]{2,1,0:T(8,128)(2,1)S(1)} %collective-permute-done.first, bf16[32,4,256,256]{3,2,1,0:T(8,128)(2,1)S(1)} %copy-done), custom_call_target="tpu_custom_call" | custom-call | flops 4600000000 | bytes 1000 | tf_op jit(solution)/shard_map/near_first/pallas_call | solution.py:209
  26.2 0.0 collective-permute-done.1.second
  26.2 0.0 collective-permute-done.2.far_second
  26.2 0.0 copy-done.5
  26.3 2.7 %near_second.1.near_field = f32[32,8,256]{2,1,0:T(8,128)S(1)} custom-call(s32[4,32]{1,0:T(4,128)S(1)} %bitcast.3, bf16[32,8,256]{2,1,0:T(8,128)(2,1)S(1)} %copy-done.2, bf16[32,8,256]{2,1,0:T(8,128)(2,1)S(1)} %collective-permute-done.first, bf16[32,8,256]{2,1,0:T(8,128)(2,1)S(1)} %collective-permute-done.1.second, ...), custom_call_target="tpu_custom_call" | custom-call | flops 4600000000 | bytes 1000 | tf_op jit(solution)/shard_map/near_second/pallas_call | solution.py:209
  29.0 5.1 %all-to-all-done.recv = bf16[128,3,8,128]{3,2,1,0:T(8,128)(2,1)S(1)} async-done(((bf16[128,3,8,128]{3,2,1,0:T(8,128)(2,1)}), bf16[128,3,8,128]{3,2,1,0:T(8,128)(2,1)S(1)}, u32[]{:S(2)}, u32[]{:S(2)}) %all-to-all-start) | async-done | bytes 786464 | tf_op jit(solution)/shard_map/all_to_all | solution.py:322
  34.1 0.0 copy-done.1
  34.1 0.0 copy-done.3
  34.1 0.0 copy-done.4
  34.1 0.0 copy-done.6
  34.2 1.7 %final.1 = f32[32,8,256]{2,1,0:T(8,128)} custom-call(s32[1,6]{1,0:T(1,128)S(1)} %copy-done.6, bf16[128,3,8,128]{3,2,1,0:T(8,128)(2,1)S(1)} %all-to-all-done.recv, f32[32,8,256]{2,1,0:T(8,128)S(1)} %near_second.1.near_field, bf16[32,64,256]{2,1,0:T(8,128)(2,1)S(1)} %copy-done.1, bf16[1,6,64,64]{3,2,1,0:T(8,128)(2,1)S(1)} %copy-done.4, ...), custom_call_target="tpu_custom_call" | custom-call | tf_op jit(solution)/shard_map/final/pallas_call | solution.py:287
  (5 shorter events, 0.0 us)
Async XLA Ops:
  0.0 10.7 %copy-start.2 = (bf16[32,8,256]{2,1,0:T(8,128)(2,1)S(1)}, bf16[32,8,256]{2,1,0:T(8,128)(2,1)}, u32[]{:S(2)}) copy-start(bf16[32,8,256]{2,1,0:T(8,128)(2,1)} %charges.2) | copy-start | bytes 393220
  0.0 10.7 %copy-start.10 = (s32[32,8]{0,1:T(8,128)S(1)}, s32[32,8]{0,1:T(8,128)}, u32[]{:S(2)}) copy-start(s32[32,8]{0,1:T(8,128)} %param.17) | copy-start | bytes 3076
  0.0 10.7 %copy-start.11 = (s32[32,8]{0,1:T(8,128)S(1)}, s32[32,8]{0,1:T(8,128)}, u32[]{:S(2)}) copy-start(s32[32,8]{0,1:T(8,128)} %param.18) | copy-start | bytes 3076
  0.0 10.7 %copy-start.8 = (bf16[32,64,256]{2,1,0:T(8,128)(2,1)S(1)}, bf16[32,64,256]{2,1,0:T(8,128)(2,1)}, u32[]{:S(2)}) copy-start(bf16[32,64,256]{2,1,0:T(8,128)(2,1)} %basis.1) | copy-start | bytes 3145732
  0.0 10.7 %copy-start.7 = (bf16[32,8,64,64]{3,2,1,0:T(8,128)(2,1)S(1)}, bf16[32,8,64,64]{3,2,1,0:T(8,128)(2,1)}, u32[]{:S(2)}) copy-start(bf16[32,8,64,64]{3,2,1,0:T(8,128)(2,1)} %couplings.2) | copy-start | bytes 6291460
  0.0 10.7 %copy-start.9 = (bf16[32,64,64]{2,1,0:T(8,128)(2,1)S(1)}, bf16[32,64,64]{2,1,0:T(8,128)(2,1)}, u32[]{:S(2)}) copy-start(bf16[32,64,64]{2,1,0:T(8,128)(2,1)} %transfer.2) | copy-start | bytes 786436
  0.0 18.1 %collective-permute-start = (bf16[32,8,256]{2,1,0:T(8,128)(2,1)}, bf16[32,8,256]{2,1,0:T(8,128)(2,1)S(1)}, u32[]{:S(2)}, u32[]{:S(2)}) collective-permute-start(bf16[32,8,256]{2,1,0:T(8,128)(2,1)} %charges.2), channel_id=1, source_target_pairs={{0,1},{2,3},{4,5},{6,7},{8,9},{10,11},{12,13},{14,15},{16,17},{18,... | collective-permute-start | bytes 393224 | tf_op jit(solution)/shard_map/ppermute | solution.py:317
  2.2 24.0 %collective-permute-start.2 = (bf16[32,8,256]{2,1,0:T(8,128)(2,1)}, bf16[32,8,256]{2,1,0:T(8,128)(2,1)S(1)}, u32[]{:S(2)}, u32[]{:S(2)}) collective-permute-start(bf16[32,8,256]{2,1,0:T(8,128)(2,1)} %charges.2), channel_id=1, source_target_pairs={{15,16},{31,32},{47,48},{63,64},{79,80},{95,96},{111,112},{16,15},... | collective-permute-start | bytes 393224 | tf_op jit(solution)/shard_map/ppermute | solution.py:317
  10.7 15.5 %copy-start.5 = (s32[32,4]{0,1:T(4,128)S(1)}, s32[32,4]{0,1:T(4,128)}, u32[]{:S(2)}) copy-start(s32[32,4]{0,1:T(4,128)} %param.13) | copy-start | bytes 1540
  13.4 20.7 %copy-start.1 = (bf16[32,64,256]{2,1,0:T(8,128)(2,1)S(1)}, bf16[32,64,256]{2,1,0:T(8,128)(2,1)}, u32[]{:S(2)}) copy-start(bf16[32,64,256]{2,1,0:T(8,128)(2,1)} %target_basis.1) | copy-start | bytes 3145732
  13.4 20.7 %copy-start.3 = (bf16[32,64,64]{2,1,0:T(8,128)(2,1)S(1)}, bf16[32,64,64]{2,1,0:T(8,128)(2,1)}, u32[]{:S(2)}) copy-start(bf16[32,64,64]{2,1,0:T(8,128)(2,1)} %transfer.3) | copy-start | bytes 786436
  13.5 20.7 %all-to-all-start = ((bf16[128,3,8,128]{3,2,1,0:T(8,128)(2,1)}), bf16[128,3,8,128]{3,2,1,0:T(8,128)(2,1)S(1)}, u32[]{:S(2)}, u32[]{:S(2)}) async-start(bf16[128,3,8,128]{3,2,1,0:T(8,128)(2,1)} %outgoing.1), calls=%async_computation | async-start | bytes 1572864 | tf_op jit(solution)/shard_map/all_to_all | solution.py:322
  17.5 8.8 %collective-permute-start.1 = (bf16[32,8,256]{2,1,0:T(8,128)(2,1)S(1)}, bf16[32,8,256]{2,1,0:T(8,128)(2,1)S(1)}, u32[]{:S(2)}, u32[]{:S(2)}) collective-permute-start(bf16[32,8,256]{2,1,0:T(8,128)(2,1)S(1)} %copy-done.2), channel_id=1, source_target_pairs={{1,2},{3,4},{5,6},{7,8},{9,10},{11,12},{13,14},{17,18},{19,20},{21... | collective-permute-start | bytes 393224 | tf_op jit(solution)/shard_map/ppermute | solution.py:323
  18.2 5.8 %copy-start = (bf16[32,4,256,256]{3,2,1,0:T(8,128)(2,1)S(1)}, bf16[32,4,256,256]{3,2,1,0:T(8,128)(2,1)}, u32[]{:S(2)}) copy-start(bf16[32,4,256,256]{3,2,1,0:T(8,128)(2,1)} %blocks.3) | copy-start | bytes 50331652
  23.9 10.2 %copy-start.4 = (bf16[1,6,64,64]{3,2,1,0:T(8,128)(2,1)S(1)}, bf16[1,6,64,64]{3,2,1,0:T(8,128)(2,1)}, u32[]{:S(2)}) copy-start(bf16[1,6,64,64]{3,2,1,0:T(8,128)(2,1)} %couplings.3) | copy-start | bytes 147460
  23.9 10.2 %copy-start.6 = (s32[1,6]{1,0:T(1,128)S(1)}, s32[1,6]{1,0:T(1,128)}, u32[]{:S(2)}) copy-start(s32[1,6]{1,0:T(1,128)} %coarse_list.1) | copy-start | bytes 76

commit v8 on v7

--- a/solution.py
+++ b/solution.py
@@ -271,15 +271,17 @@
     coarse = ((coarse[0] + coarse[1]) + (coarse[2] + coarse[3])) + (coarse[4] + coarse[5])
     lowered = dot(coarse.astype(BF16), transfer[...].reshape(LEAVES * RANK, RANK), NT)
     upper = iota((RHS, 128), 0) < 4
+    low = iota((RHS, 128), 1) < RANK
     for l in range(0, LEAVES, 2):
         rows = far[l * 4 : l * 4 + 8, :]
-        swapped = pltpu.roll(rows, RANK, 1)
-        turned = pltpu.roll(rows, 4, 0)
+        turned = pltpu.roll(pltpu.roll(rows, RANK, 1), 4, 0)
         pair = lowered[:, l * RANK : (l + 2) * RANK]
-        even = jnp.where(upper, rows, pltpu.roll(swapped, 4, 0)) + pair
-        odd = jnp.where(upper, turned, swapped) + pltpu.roll(pair, RANK, 1)
-        for i, local in enumerate((even, odd)):
-            out[l + i] = near_field[l + i] + dot(local[:, :RANK].astype(BF16), target_basis[l + i])
+        even = jnp.where(low, jnp.where(upper, rows, turned) + pair, 0.0)
+        odd = jnp.where(low, 0.0, jnp.where(upper, turned, rows) + pair)
+        local = jnp.concatenate([even, odd], axis=0).astype(BF16)
+        product = dot(local, target_basis[l : l + 2].reshape(2 * RANK, POINTS))
+        out[l] = near_field[l] + product[:RHS]
+        out[l + 1] = near_field[l + 1] + product[RHS:]
 
 
 def final(coarse_list, recv, near_field, target_basis, coarse_couplings, down_transfer):

time: 36.1 us -> 36 us (level)
  no operation moved by 1% of the time
where the time goes in v8:
time: 36 us; the launch traced here: 35.8 us
  starting transfers between devices  15.3 us (42%)
  Pallas kernels  9.39 us (26%)
  local copies, waits for them, and re-layouts  5.83 us (16%)
  waiting for transfers between devices  5.12 us (14%)
    ppermute x2, starting transfers between devices, body(): lax.ppermute(charges, AXES, some + [(j, i) for i, j in some])  10.6 us
    unnamed x24, local copies, waits for them, and re-layouts  5.83 us
    all_to_all x1, waiting for transfers between devices, body(): recv = lax.all_to_all(send, AXES, 0, 0, tiled=True)  5.12 us
    pallas_call x2, Pallas kernels, near(): pl.pallas_call(kernel, out_shape=jax.ShapeDtypeStruct((LEAVES, RHS, POINT...  5.04 us
    all_to_all x1, starting transfers between devices, body(): recv = lax.all_to_all(send, AXES, 0, 0, tiled=True)  4.01 us
    pallas_call x1, Pallas kernels, outgoing(): pl.pallas_call(outgoing_kernel, out_shape=jax.ShapeDtypeStruct((DEVICES,...  2.7 us
    pallas_call x1, Pallas kernels, final(): pl.pallas_call(final_kernel, out_shape=jax.ShapeDtypeStruct((LEAVES, RHS,...  1.63 us
  transfers between devices with their start and end apart: 4, of which 1 were waited for; matrix products, arithmetic and copies ran while one was open for 0% of the time, Pallas kernels for 22%

profile of v8, /device:TPU:1, one launch (start us, length us, event | category | flops | bytes accessed | tf_op | source)
XLA Modules:
  0.0 35.8 jit_solution(11270722925574076317)
XLA Ops:
  0.0 0.0 copy-start.2
  0.0 0.0 copy-start.8
  0.0 0.0 copy-start.7
  0.0 0.0 copy-start.9
  0.0 2.2 %collective-permute-start = (bf16[32,8,256]{2,1,0:T(8,128)(2,1)}, bf16[32,8,256]{2,1,0:T(8,128)(2,1)S(1)}, u32[]{:S(2)}, u32[]{:S(2)}) collective-permute-start(bf16[32,8,256]{2,1,0:T(8,128)(2,1)} %charges.2), channel_id=1, source_target_pairs={{0,1},{2,3},{4,5},{6,7},{8,9},{10,11},{12,13},{14,15},{16,17},{18,... | collective-permute-start | bytes 393224 | tf_op jit(solution)/shard_map/ppermute | solution.py:319
  2.2 8.4 %collective-permute-start.2 = (bf16[32,8,256]{2,1,0:T(8,128)(2,1)}, bf16[32,8,256]{2,1,0:T(8,128)(2,1)S(1)}, u32[]{:S(2)}, u32[]{:S(2)}) collective-permute-start(bf16[32,8,256]{2,1,0:T(8,128)(2,1)} %charges.2), channel_id=1, source_target_pairs={{15,16},{31,32},{47,48},{63,64},{79,80},{95,96},{111,112},{16,15},... | collective-permute-start | bytes 393224 | tf_op jit(solution)/shard_map/ppermute | solution.py:319
  10.7 0.0 copy-done.2
  10.7 0.0 copy-done.10
  10.7 0.0 copy-done.11
  10.7 0.0 copy-done.8
  10.7 0.0 copy-done.7
  10.7 0.0 copy-done.9
  10.7 0.0 copy-start.5
  10.7 2.7 %outgoing.1 = bf16[128,3,8,128]{3,2,1,0:T(8,128)(2,1)} custom-call(bf16[256,256]{1,0:T(8,128)(2,1)S(1)} %triangle.1.earlier, s32[8,32]{1,0:T(8,128)S(1)} %bitcast.4, s32[8,32]{1,0:T(8,128)S(1)} %bitcast.5, bf16[32,8,256]{2,1,0:T(8,128)(2,1)S(1)} %copy-done.2, bf16[32,64,256]{2,1,0:T(8,128)(2,1)S(1)} %copy-done.8, bf16[32,8,64,64]{3,2,1,0:T(8,128)(2,1)S(1)} %copy-done.7, ...), custom_call_target="tpu_custom_call" | custom-call | flops 26843545600 | bytes 1000 | tf_op jit(solution)/shard_map/outgoing/pallas_call | solution.py:148
  13.4 0.0 copy-start.1
  13.4 0.0 copy-start.3
  13.5 4.0 %all-to-all-start = ((bf16[128,3,8,128]{3,2,1,0:T(8,128)(2,1)}), bf16[128,3,8,128]{3,2,1,0:T(8,128)(2,1)S(1)}, u32[]{:S(2)}, u32[]{:S(2)}) async-start(bf16[128,3,8,128]{3,2,1,0:T(8,128)(2,1)} %outgoing.1), calls=%async_computation | async-start | bytes 1572864 | tf_op jit(solution)/shard_map/all_to_all | solution.py:324
  17.5 0.7 %collective-permute-start.1 = (bf16[32,8,256]{2,1,0:T(8,128)(2,1)S(1)}, bf16[32,8,256]{2,1,0:T(8,128)(2,1)S(1)}, u32[]{:S(2)}, u32[]{:S(2)}) collective-permute-start(bf16[32,8,256]{2,1,0:T(8,128)(2,1)S(1)} %copy-done.2), channel_id=1, source_target_pairs={{1,2},{3,4},{5,6},{7,8},{9,10},{11,12},{13,14},{17,18},{19,20},{21... | collective-permute-start | bytes 393224 | tf_op jit(solution)/shard_map/ppermute | solution.py:325
  18.2 0.0 collective-permute-done.first
  18.2 0.0 copy-start
  18.2 5.8 %copy-done = bf16[32,4,256,256]{3,2,1,0:T(8,128)(2,1)S(1)} copy-done((bf16[32,4,256,256]{3,2,1,0:T(8,128)(2,1)S(1)}, bf16[32,4,256,256]{3,2,1,0:T(8,128)(2,1)}, u32[]{:S(2)}) %copy-start) | copy-done | bytes 16777240
  23.9 2.3 %near_first.1.partial = f32[32,8,256]{2,1,0:T(8,128)S(1)} custom-call(bf16[32,8,256]{2,1,0:T(8,128)(2,1)S(1)} %copy-done.2, bf16[32,8,256]{2,1,0:T(8,128)(2,1)S(1)} %collective-permute-done.first, bf16[32,4,256,256]{3,2,1,0:T(8,128)(2,1)S(1)} %copy-done), custom_call_target="tpu_custom_call" | custom-call | flops 4600000000 | bytes 1000 | tf_op jit(solution)/shard_map/near_first/pallas_call | solution.py:209
  26.2 0.0 collective-permute-done.1.second
  26.2 0.0 collective-permute-done.2.far_second
  26.2 0.0 copy-done.5
  26.3 2.8 %near_second.1.near_field = f32[32,8,256]{2,1,0:T(8,128)S(1)} custom-call(s32[4,32]{1,0:T(4,128)S(1)} %bitcast.3, bf16[32,8,256]{2,1,0:T(8,128)(2,1)S(1)} %copy-done.2, bf16[32,8,256]{2,1,0:T(8,128)(2,1)S(1)} %collective-permute-done.first, bf16[32,8,256]{2,1,0:T(8,128)(2,1)S(1)} %collective-permute-done.1.second, ...), custom_call_target="tpu_custom_call" | custom-call | flops 4600000000 | bytes 1000 | tf_op jit(solution)/shard_map/near_second/pallas_call | solution.py:209
  29.0 5.1 %all-to-all-done.recv = bf16[128,3,8,128]{3,2,1,0:T(8,128)(2,1)S(1)} async-done(((bf16[128,3,8,128]{3,2,1,0:T(8,128)(2,1)}), bf16[128,3,8,128]{3,2,1,0:T(8,128)(2,1)S(1)}, u32[]{:S(2)}, u32[]{:S(2)}) %all-to-all-start) | async-done | bytes 786464 | tf_op jit(solution)/shard_map/all_to_all | solution.py:324
  34.1 0.0 copy-done.1
  34.1 0.0 copy-done.3
  34.1 0.0 copy-done.4
  34.1 0.0 copy-done.6
  34.2 1.6 %final.1 = f32[32,8,256]{2,1,0:T(8,128)} custom-call(s32[1,6]{1,0:T(1,128)S(1)} %copy-done.6, bf16[128,3,8,128]{3,2,1,0:T(8,128)(2,1)S(1)} %all-to-all-done.recv, f32[32,8,256]{2,1,0:T(8,128)S(1)} %near_second.1.near_field, bf16[32,64,256]{2,1,0:T(8,128)(2,1)S(1)} %copy-done.1, bf16[1,6,64,64]{3,2,1,0:T(8,128)(2,1)S(1)} %copy-done.4, ...), custom_call_target="tpu_custom_call" | custom-call | tf_op jit(solution)/shard_map/final/pallas_call | solution.py:289
  (5 shorter events, 0.0 us)
Async XLA Ops:
  0.0 10.7 %copy-start.2 = (bf16[32,8,256]{2,1,0:T(8,128)(2,1)S(1)}, bf16[32,8,256]{2,1,0:T(8,128)(2,1)}, u32[]{:S(2)}) copy-start(bf16[32,8,256]{2,1,0:T(8,128)(2,1)} %charges.2) | copy-start | bytes 393220
  0.0 10.7 %copy-start.10 = (s32[32,8]{0,1:T(8,128)S(1)}, s32[32,8]{0,1:T(8,128)}, u32[]{:S(2)}) copy-start(s32[32,8]{0,1:T(8,128)} %param.17) | copy-start | bytes 3076
  0.0 10.7 %copy-start.11 = (s32[32,8]{0,1:T(8,128)S(1)}, s32[32,8]{0,1:T(8,128)}, u32[]{:S(2)}) copy-start(s32[32,8]{0,1:T(8,128)} %param.18) | copy-start | bytes 3076
  0.0 10.7 %copy-start.8 = (bf16[32,64,256]{2,1,0:T(8,128)(2,1)S(1)}, bf16[32,64,256]{2,1,0:T(8,128)(2,1)}, u32[]{:S(2)}) copy-start(bf16[32,64,256]{2,1,0:T(8,128)(2,1)} %basis.1) | copy-start | bytes 3145732
  0.0 10.7 %copy-start.7 = (bf16[32,8,64,64]{3,2,1,0:T(8,128)(2,1)S(1)}, bf16[32,8,64,64]{3,2,1,0:T(8,128)(2,1)}, u32[]{:S(2)}) copy-start(bf16[32,8,64,64]{3,2,1,0:T(8,128)(2,1)} %couplings.2) | copy-start | bytes 6291460
  0.0 10.7 %copy-start.9 = (bf16[32,64,64]{2,1,0:T(8,128)(2,1)S(1)}, bf16[32,64,64]{2,1,0:T(8,128)(2,1)}, u32[]{:S(2)}) copy-start(bf16[32,64,64]{2,1,0:T(8,128)(2,1)} %transfer.2) | copy-start | bytes 786436
  0.0 18.1 %collective-permute-start = (bf16[32,8,256]{2,1,0:T(8,128)(2,1)}, bf16[32,8,256]{2,1,0:T(8,128)(2,1)S(1)}, u32[]{:S(2)}, u32[]{:S(2)}) collective-permute-start(bf16[32,8,256]{2,1,0:T(8,128)(2,1)} %charges.2), channel_id=1, source_target_pairs={{0,1},{2,3},{4,5},{6,7},{8,9},{10,11},{12,13},{14,15},{16,17},{18,... | collective-permute-start | bytes 393224 | tf_op jit(solution)/shard_map/ppermute | solution.py:319
  2.2 24.0 %collective-permute-start.2 = (bf16[32,8,256]{2,1,0:T(8,128)(2,1)}, bf16[32,8,256]{2,1,0:T(8,128)(2,1)S(1)}, u32[]{:S(2)}, u32[]{:S(2)}) collective-permute-start(bf16[32,8,256]{2,1,0:T(8,128)(2,1)} %charges.2), channel_id=1, source_target_pairs={{15,16},{31,32},{47,48},{63,64},{79,80},{95,96},{111,112},{16,15},... | collective-permute-start | bytes 393224 | tf_op jit(solution)/shard_map/ppermute | solution.py:319
  10.7 15.5 %copy-start.5 = (s32[32,4]{0,1:T(4,128)S(1)}, s32[32,4]{0,1:T(4,128)}, u32[]{:S(2)}) copy-start(s32[32,4]{0,1:T(4,128)} %param.13) | copy-start | bytes 1540
  13.4 20.7 %copy-start.1 = (bf16[32,64,256]{2,1,0:T(8,128)(2,1)S(1)}, bf16[32,64,256]{2,1,0:T(8,128)(2,1)}, u32[]{:S(2)}) copy-start(bf16[32,64,256]{2,1,0:T(8,128)(2,1)} %target_basis.1) | copy-start | bytes 3145732
  13.4 20.7 %copy-start.3 = (bf16[32,64,64]{2,1,0:T(8,128)(2,1)S(1)}, bf16[32,64,64]{2,1,0:T(8,128)(2,1)}, u32[]{:S(2)}) copy-start(bf16[32,64,64]{2,1,0:T(8,128)(2,1)} %transfer.3) | copy-start | bytes 786436
  13.5 20.7 %all-to-all-start = ((bf16[128,3,8,128]{3,2,1,0:T(8,128)(2,1)}), bf16[128,3,8,128]{3,2,1,0:T(8,128)(2,1)S(1)}, u32[]{:S(2)}, u32[]{:S(2)}) async-start(bf16[128,3,8,128]{3,2,1,0:T(8,128)(2,1)} %outgoing.1), calls=%async_computation | async-start | bytes 1572864 | tf_op jit(solution)/shard_map/all_to_all | solution.py:324
  17.5 8.8 %collective-permute-start.1 = (bf16[32,8,256]{2,1,0:T(8,128)(2,1)S(1)}, bf16[32,8,256]{2,1,0:T(8,128)(2,1)S(1)}, u32[]{:S(2)}, u32[]{:S(2)}) collective-permute-start(bf16[32,8,256]{2,1,0:T(8,128)(2,1)S(1)} %copy-done.2), channel_id=1, source_target_pairs={{1,2},{3,4},{5,6},{7,8},{9,10},{11,12},{13,14},{17,18},{19,20},{21... | collective-permute-start | bytes 393224 | tf_op jit(solution)/shard_map/ppermute | solution.py:325
  18.2 5.8 %copy-start = (bf16[32,4,256,256]{3,2,1,0:T(8,128)(2,1)S(1)}, bf16[32,4,256,256]{3,2,1,0:T(8,128)(2,1)}, u32[]{:S(2)}) copy-start(bf16[32,4,256,256]{3,2,1,0:T(8,128)(2,1)} %blocks.3) | copy-start | bytes 50331652
  23.9 10.2 %copy-start.4 = (bf16[1,6,64,64]{3,2,1,0:T(8,128)(2,1)S(1)}, bf16[1,6,64,64]{3,2,1,0:T(8,128)(2,1)}, u32[]{:S(2)}) copy-start(bf16[1,6,64,64]{3,2,1,0:T(8,128)(2,1)} %couplings.3) | copy-start | bytes 147460
  23.9 10.2 %copy-start.6 = (s32[1,6]{1,0:T(1,128)S(1)}, s32[1,6]{1,0:T(1,128)}, u32[]{:S(2)}) copy-start(s32[1,6]{1,0:T(1,128)} %coarse_list.1) | copy-start | bytes 76
